TPU v7x, 128 devices: a whole 4x4x4 slice. The times are simulated.
128 devices in a mesh: dp: 8 (over z, core), tensor: 16 (over y, x).
Axes of the slice: x: 4, y: 4, z: 4, core: 2. Of those that a mesh axis runs over, the one named last changes fastest.
Arguments:
- tokens: bfloat16 [10240, 4096], P('dp'), may hold values from -6 to 6
- gate_weight: bfloat16 [4096, 14336], P(None, 'tensor'), may hold values from -0.125 to 0.125
- up_values: bfloat16 [10240, 14336], P('dp', 'tensor'), may hold values from -6 to 6
- hidden_grad: bfloat16 [10240, 14336], P('dp', 'tensor'), may hold values from -48 to 48
- log_ratios: float32 [64, 2], P('dp'), may hold values from -60 to 60
- q_factors: float32 [14336, 32], P('tensor'), may hold values from -6 to 6
- error_feedback: bfloat16 [8, 4096, 14336], P('dp', None, 'tensor'), may hold values from -12 to 12
Outputs:
- token_grad: bfloat16 [10240, 4096], P('dp', 'tensor')
- q_next: float32 [14336, 32], P('tensor')
- error_next: bfloat16 [8, 4096, 14336], P('dp', None, 'tensor')
All inputs are finite; a program needn't handle non-finite values.
Results may differ from a plain program's by a relative error of at most 0.019.
Values may be sent and summed in bfloat16 or wider, within the bound.
No kernel may reach another device: no remote copies, remote signals or barrier semaphores. Data moves between devices by JAX's collectives and lax.ppermute only.
A program may use at most 192 MiB of HBM per device.

v0:
```python
import jax
import jax.numpy as jnp
from jax import lax
from jax.sharding import PartitionSpec as P

LEN = 80


dpo_beta = 0.1
highest = lax.Precision.HIGHEST


def pair_weights(log_ratios, seq_len):
    margin = dpo_beta * (log_ratios[:, 0] - log_ratios[:, 1])
    scaled = dpo_beta * jax.nn.sigmoid(-margin)
    signed = jnp.stack([-scaled, scaled], axis=1)
    spread = jnp.broadcast_to(signed[:, :, None], signed.shape + (seq_len,))
    return spread.reshape(-1)


def orthonormal(left_sum, gram_matrix):
    lower_factor = jnp.linalg.cholesky(gram_matrix)
    return lax.linalg.triangular_solve(
        lower_factor, left_sum, left_side=False, lower=True, transpose_a=True
    )


def shards(tokens, gate_weight, up_values, hidden_grad, log_ratios, q_factors, error_feedback):
    replicas = lax.axis_size("dp")
    contract_rows = (((0,), (0,)), ((), ()))
    row_weight = pair_weights(log_ratios, LEN)
    gate_pre = jnp.dot(tokens, gate_weight, preferred_element_type=jnp.float32)
    sigmoid_gate = jax.nn.sigmoid(gate_pre)
    silu_slope = sigmoid_gate * (1.0 + gate_pre * (1.0 - sigmoid_gate))
    gate_grad = (
        row_weight[:, None]
        * hidden_grad.astype(jnp.float32)
        * up_values.astype(jnp.float32)
        * silu_slope
    ).astype(jnp.bfloat16)
    partial_input = lax.dot_general(
        gate_grad, gate_weight, (((1,), (1,)), ((), ())), preferred_element_type=jnp.float32
    )
    partial_input = partial_input.astype(jnp.bfloat16).astype(jnp.float32)
    token_grad = lax.psum_scatter(
        partial_input.astype(jnp.bfloat16), "tensor", scatter_dimension=1, tiled=True
    )
    weight_grad = lax.dot_general(
        tokens, gate_grad, contract_rows, preferred_element_type=jnp.float32
    )
    combined = weight_grad + error_feedback[0].astype(jnp.float32)
    merged_half = combined.astype(jnp.bfloat16)
    q_half = q_factors.astype(jnp.bfloat16)
    left_local = jnp.dot(merged_half, q_half, preferred_element_type=jnp.float32)
    left_sum = lax.psum(left_local.astype(jnp.bfloat16), "dp").astype(jnp.float32) / replicas
    gram_matrix = jnp.dot(left_sum.T, left_sum, precision=highest)
    left_ortho = orthonormal(left_sum, gram_matrix).astype(jnp.bfloat16)
    right_local = lax.dot_general(
        merged_half, left_ortho, contract_rows, preferred_element_type=jnp.float32
    )
    q_next = lax.psum(right_local.astype(jnp.bfloat16), "dp").astype(jnp.float32) / replicas
    q_round = q_next.astype(jnp.bfloat16)
    approx = lax.dot_general(
        left_ortho, q_round, (((1,), (1,)), ((), ())), preferred_element_type=jnp.float32
    )
    error_next = (combined - approx).astype(jnp.bfloat16)
    return (token_grad, q_next, error_next[None])


def solution(mesh):
    return jax.shard_map(
        shards,
        mesh=mesh,
        in_specs=(
            P("dp", None),
            P(None, "tensor"),
            P("dp", "tensor"),
            P("dp", "tensor"),
            P("dp", None),
            P("tensor", None),
            P("dp", None, "tensor"),
        ),
        out_specs=(P("dp", "tensor"), P("tensor", None), P("dp", None, "tensor")),
        check_vma=False,
    )
```

profile of v0, /device:TPU:1, one launch (start us, length us, event | category | flops | bytes accessed | tf_op | source)
XLA Modules:
  0.0 203.0 jit_solution(4386447929637810100)
XLA Ops:
  8.0 0.0 all-reduce.2.cloned.1.call-start
  8.0 0.8 fusion.21
  8.8 0.1 copy.10
  8.9 0.1 broadcast_in_dim.6
  9.0 0.1 mul.34
  9.1 10.8 %copy.11 = bf16[1,4096,896]{1,2,0:T(8,128)(2,1)} copy(bf16[1,4096,896]{2,1,0:T(8,128)(2,1)} %param.13) | data formatting | bytes 14680064 | tf_op args[6]
  19.9 0.0 copy-start.3
  19.9 17.3 %fusion.22 = f32[1280,896]{1,0:T(8,128)} fusion(bf16[1280,4096]{1,0:T(8,128)(2,1)} %param.7, bf16[4096,896]{1,0:T(8,128)(2,1)} %param.8), kind=kOutput, calls=%fused_computation.37 | convolution fusion | flops 9395240960 | bytes 22413312 | tf_op jit(solution)/shard_map/dot_general | solution.py:32
  37.2 0.0 copy-done.3
  37.2 0.0 copy-start.2
  37.2 17.5 %fusion.2 = f32[896,4096]{1,0:T(8,128)S(1)} fusion(bf16[1280,4096]{1,0:T(8,128)(2,1)} %param.7, f32[1280,896]{1,0:T(8,128)} %fusion.22, bf16[1280,896]{1,0:T(8,128)(2,1)S(1)} %copy-done.3, bf16[1280,896]{1,0:T(8,128)(2,1)} %param.10, f32[1280]{0:T(1024)S(1)} %mul.34), kind=kOutput, calls=%fused_computation.8 | convolution fusion | flops 9410150400 | bytes 34345984 | tf_op jit(solution)/shard_map/dot_general | solution.py:48
  54.7 0.0 copy-start
  54.7 5.2 %copy-done = f32[896,4096]{1,0:T(8,128)} copy-done((f32[896,4096]{1,0:T(8,128)}, f32[896,4096]{1,0:T(8,128)S(1)}, u32[]{:S(2)}) %copy-start) | copy-done | bytes 14680088
  59.9 0.0 copy-done.2
  59.9 5.6 %convolution_convert_fusion.1 = bf16[4096,32]{0,1:T(8,128)(2,1)} fusion(f32[896,32]{0,1:T(8,128)S(1)} %copy-done.2, f32[896,4096]{1,0:T(8,128)S(1)} %fusion.2, bf16[1,4096,896]{1,2,0:T(8,128)(2,1)} %copy.11), kind=kOutput, calls=%fused_computation.6 | convolution fusion | flops 246050816 | bytes 22396928 | tf_op jit(solution)/shard_map/dot_general | solution.py:54
  65.6 0.0 all-reduce.2.cloned.1.call-update
  65.6 0.2 reduce-scatter.2.cloned.1.call-start
  65.8 20.5 %convolution_convert_fusion = bf16[1280,4096]{1,0:T(8,128)(2,1)} fusion(bf16[4096,896]{1,0:T(8,128)(2,1)} %param.8, f32[1280,896]{1,0:T(8,128)} %fusion.22, bf16[1280,896]{1,0:T(8,128)(2,1)S(1)} %copy-done.3, bf16[1280,896]{1,0:T(8,128)(2,1)} %param.10, f32[1280]{0:T(1024)S(1)} %mul.34), kind=kOutput, calls=%fused_computation | convolution fusion | flops 9415393280 | bytes 27005952 | tf_op jit(solution)/shard_map/dot_general | solution.py:41
  86.3 0.0 reduce-scatter.2.cloned.1.call-update
  86.3 41.2 %all-reduce.2.cloned.1.call-done = bf16[4096,32]{0,1:T(8,128)(2,1)} async-done(((bf16[4096,32]{0,1:T(8,128)(2,1)}), bf16[4096,32]{0,1:T(8,128)(2,1)}) %all-reduce.2.cloned.1.call-update) | async-done | bytes 262160 | tf_op jit(solution)/shard_map/psum | solution.py:55
  127.6 1.6 fusion.7
  129.2 0.1 copy.12
  129.3 2.9 %cholesky.16 = f32[32,32]{1,0:T(8,128)S(1)} custom-call(f32[32,32]{1,0:T(8,128)S(1)} %fusion.14), custom_call_target="Cholesky" | custom-call | tf_op jit(solution)/shard_map/jit(cholesky)/cholesky | solution.py:22
  132.2 0.6 compare_reduce_fusion
  132.9 0.7 fusion.12
  133.6 2.4 %custom-call.6 = f32[1,32,32]{1,2,0:T(8,128)S(1)} custom-call(f32[1,32,32]{2,1,0:T(8,128)S(1)} %fusion.12), custom_call_target="InvertDiagBlocksLowerTriangular" | custom-call | tf_op jit(solution)/shard_map/triangular_solve | solution.py:23
  136.0 1.6 convolution_convert_fusion.2
  137.6 10.0 %convolution_convert_fusion.3 = bf16[896,32]{0,1:T(8,128)(2,1)S(1)} fusion(bf16[4096,32]{0,1:T(8,128)(2,1)S(1)} %convolution_convert_fusion.2, f32[896,4096]{1,0:T(8,128)} %copy-done, bf16[1,4096,896]{1,2,0:T(8,128)(2,1)} %copy.11), kind=kOutput, calls=%fused_computation.13 | convolution fusion | flops 245919744 | bytes 22339584 | tf_op jit(solution)/shard_map/dot_general | solution.py:58
  147.6 25.1 %psum.15 = bf16[896,32]{0,1:T(8,128)(2,1)S(1)} all-reduce(bf16[896,32]{0,1:T(8,128)(2,1)S(1)} %convolution_convert_fusion.3), channel_id=1, replica_groups=mesh['dp'=8,'tensor'=16] {'dp'}, use_global_device_ids=true, to_apply=%region_4.5 | all-reduce | flops 28672 | bytes 114688 | tf_op jit(solution)/shard_map/psum | solution.py:61
  172.8 0.0 copy-start.1
  172.8 12.0 %fusion.1 = bf16[1,4096,896]{1,2,0:T(8,128)(2,1)} fusion(bf16[4096,32]{0,1:T(8,128)(2,1)S(1)} %convolution_convert_fusion.2, bf16[1,4096,896]{1,2,0:T(8,128)(2,1)} %copy.11, f32[896,4096]{1,0:T(8,128)} %copy-done, f32[896,32]{0,1:T(8,128)S(1)} %convert_multiply_fusion.3), kind=kOutput, calls=%fused_computation.4 | convolution fusion | flops 249589760 | bytes 29736960 | tf_op jit(solution)/shard_map/dot_general | solution.py:63
  184.8 0.0 copy-done.1
  184.8 10.8 %copy.14 = bf16[1,4096,896]{2,1,0:T(8,128)(2,1)} copy(bf16[1,4096,896]{1,2,0:T(8,128)(2,1)} %fusion.1) | data formatting | bytes 14680064
  195.6 0.0 reduce-scatter.2.cloned.1.call-done
  (4 shorter events, 0.1 us)
Async XLA Ops:
  8.0 119.6 %all-reduce.2.cloned.1.call-start = ((), (), s32[]{:S(2)}) async-start(), calls=%async_computation.2 | async-start | bytes 524288 | tf_op jit(solution)/shard_map/psum | solution.py:55
  19.9 17.3 %copy-start.3 = (bf16[1280,896]{1,0:T(8,128)(2,1)S(1)}, bf16[1280,896]{1,0:T(8,128)(2,1)}, u32[]{:S(2)}) copy-start(bf16[1280,896]{1,0:T(8,128)(2,1)} %param.9) | copy-start | bytes 6881284
  37.2 22.7 %copy-start.2 = (f32[896,32]{0,1:T(8,128)S(1)}, f32[896,32]{0,1:T(8,128)}, u32[]{:S(2)}) copy-start(f32[896,32]{0,1:T(8,128)} %param.12) | copy-start | bytes 344068
  54.7 5.2 %copy-start = (f32[896,4096]{1,0:T(8,128)}, f32[896,4096]{1,0:T(8,128)S(1)}, u32[]{:S(2)}) copy-start(f32[896,4096]{1,0:T(8,128)S(1)} %fusion.2) | copy-start | bytes 44040196
  65.6 130.0 %reduce-scatter.2.cloned.1.call-start = ((), (), s32[]{:S(2)}) async-start(), calls=%async_computation.1 | async-start | bytes 11141120 | tf_op jit(solution)/shard_map/reduce_scatter | solution.py:45
  172.8 12.0 %copy-start.1 = (f32[896,32]{0,1:T(8,128)}, f32[896,32]{0,1:T(8,128)S(1)}, u32[]{:S(2)}) copy-start(f32[896,32]{0,1:T(8,128)S(1)} %convert_multiply_fusion.3) | copy-start | bytes 344068
Sparse Core Ops, SparseCore 0:
  65.7 61.7 all-reduce.1
Sparse Core Ops, SparseCore 1:
  86.4 91.9 reduce-scatter.1
where the time goes:
time: 205 us; the launch traced here: 203 us
  matrix products  86.2 us (42%)
  waiting for transfers between devices  41.3 us (20%)
  local copies, waits for them, and re-layouts  27.1 us (13%)
  blocking collectives  25.1 us (12%)
  between operations  15.5 us (8%)
  other arithmetic  7.48 us (4%)
    psum x1, waiting for transfers between devices, shards(): lax.psum(left_local.astype(jnp.bfloat16), 'dp').astype(jnp.float32)  41.2 us
    unnamed x10, local copies, waits for them, and re-layouts  26.8 us
    psum x1, blocking collectives, shards(): lax.psum(right_local.astype(jnp.bfloat16), 'dp').astype(jnp.float32)  25.1 us
    dot_general x1, matrix products, shards(): lax.dot_general(gate_grad, gate_weight, (((1,), (1,)), ((), ())), preferr...  20.5 us
    dot_general x1, matrix products, shards(): lax.dot_general(tokens, gate_grad, contract_rows, preferred_element_type=...  17.5 us
    dot_general x1, matrix products, shards(): gate_pre = jnp.dot(tokens, gate_weight, preferred_element_type=jnp.float32)  17.3 us
    dot_general x1, matrix products, shards(): lax.dot_general(left_ortho, q_round, (((1,), (1,)), ((), ())), preferred_...  12 us
    dot_general x1, matrix products, shards(): lax.dot_general(merged_half, left_ortho, contract_rows, preferred_element...  10 us
  transfers between devices with their start and end apart: 2, of which 1 were waited for; matrix products, arithmetic and copies ran while one was open for 31% of the time, Pallas kernels for 0%

commit v1 on v0

v1 whole, which is shorter than its diff:
```python
import functools

import jax
import jax.numpy as jnp
from jax import lax
from jax.experimental import pallas as pl
from jax.experimental.pallas import tpu as pltpu
from jax.sharding import PartitionSpec as P

bf16 = jnp.bfloat16
f32 = jnp.float32
MIB = 1 << 20

LEN = 80
PAIR = 2 * LEN
ROWS = 1280
ROWS_A = 640
D = 4096
WIDE = 896
OUT = 256
R = 32
SIDE = 4

dpo_beta = 0.1
highest = lax.Precision.HIGHEST
NT = (((1,), (1,)), ((), ()))
TN = (((0,), (0,)), ((), ()))
NN = (((1,), (0,)), ((), ()))

VM = pl.BlockSpec(memory_space=pltpu.VMEM)
SM = pl.BlockSpec(memory_space=pltpu.SMEM)
ANY = pl.BlockSpec(memory_space=pl.ANY)
HBM = pl.BlockSpec(memory_space=pltpu.HBM)


def params(mib):
    return pltpu.CompilerParams(vmem_limit_bytes=mib * MIB)


LITTLE = pl.CostEstimate(flops=1, bytes_accessed=1, transcendentals=0)


def skipping(body, n, more):
    return lambda *refs: body(*refs[:n], *refs[n + more :])


def dot(a, b, dims):
    return lax.dot_general(a, b, dims, preferred_element_type=f32)


CHUNK = 512
TILE = 2 * PAIR
DEST = SIDE * OUT
GROUPS = (("x", 0, ROWS_A), ("y", ROWS_A, ROWS - ROWS_A))
FAR, NEAR, OWN = range(3)


def position(kind, axis, place_ref):
    me = place_ref[0 if axis == "x" else 1]
    core = place_ref[2]
    return lax.rem(me + (2, 1 + 2 * core, 0)[kind], SIDE)


def weights_for(axis, c, weight_ref):
    if axis == "y":
        return weight_ref[pl.ds(pl.multiple_of(c * DEST, DEST), DEST), :]
    return jnp.concatenate(
        [weight_ref[pl.ds(feature_block(axis, j, c), OUT), :] for j in range(SIDE)], axis=0
    )


def put_terms(kind, place_ref, grad_ref, weight_ref, outs):
    for (axis, base, n), out_ref in zip(GROUPS, outs):
        weight = weights_for(axis, position(kind, axis, place_ref), weight_ref)
        term = dot(grad_ref[base : base + n, :], weight, NT).astype(bf16)
        for j in range(SIDE):
            out_ref[j] = term[:, j * OUT : (j + 1) * OUT]


def feature_block(axis, j, c):
    return pl.multiple_of((j * SIDE + c if axis == "x" else c * SIDE + j) * OUT, OUT)


def gate_grad_of(pair, ratio_ref, gate_pre, hidden, up):
    margin = dpo_beta * (ratio_ref[0, pair] - ratio_ref[1, pair])
    scaled = dpo_beta * jax.nn.sigmoid(jnp.full((PAIR, 1), -margin, f32))
    chosen = lax.broadcasted_iota(jnp.int32, (PAIR, 1), 0) < LEN
    row_weight = jnp.where(chosen, -scaled, scaled)
    s = jax.nn.sigmoid(gate_pre)
    slope = s * (1.0 + gate_pre * (1.0 - s))
    return (row_weight * hidden.astype(f32) * up.astype(f32) * slope).astype(bf16)


def gate_body(
    place_ref, ratio_ref, token_ref, weight_hbm, hidden_ref, up_ref,
    grad_ref, far_x, far_y, weight_ref, pre_ref, sems,
):
    i = pl.program_id(0)

    def chunk(k):
        at = pl.ds(k * CHUNK, CHUNK)
        return pltpu.make_async_copy(weight_hbm.at[at], weight_ref.at[at], sems.at[k])

    def finish(gate_pre):
        for p in range(TILE // PAIR):
            at = slice(p * PAIR, (p + 1) * PAIR)
            row = pl.multiple_of(i * TILE + p * PAIR, PAIR)
            grad_ref[pl.ds(row, PAIR)] = gate_grad_of(
                i * (TILE // PAIR) + p, ratio_ref, gate_pre[at], hidden_ref[at], up_ref[at]
            )

    @pl.when(i == 0)
    def _():
        for k in range(D // CHUNK):
            chunk(k).start()
        for k in range(D // CHUNK):
            chunk(k).wait()
            at = slice(k * CHUNK, (k + 1) * CHUNK)
            part = dot(token_ref[:, at], weight_ref[at], NN)
            if k == 0:
                pre_ref[...] = part
            elif k < D // CHUNK - 1:
                pre_ref[...] += part
            else:
                finish(pre_ref[...] + part)

    @pl.when(i > 0)
    def _():
        finish(dot(token_ref[...], weight_ref[...], NN))

    @pl.when(i == ROWS // TILE - 1)
    def _():
        put_terms(FAR, place_ref, grad_ref, weight_ref, (far_x, far_y))


def messages():
    return [jax.ShapeDtypeStruct((SIDE, n, OUT), bf16) for _, _, n in GROUPS]


def gate(place, ratios, tokens, weight, hidden, up):
    rows = lambda wide: pl.BlockSpec((TILE, wide), lambda i: (i, 0))
    return pl.pallas_call(
        gate_body,
        grid=(ROWS // TILE,),
        in_specs=[SM, SM, rows(D), HBM, rows(WIDE), rows(WIDE)],
        out_specs=[VM] * 4,
        out_shape=[jax.ShapeDtypeStruct((ROWS, WIDE), bf16), *messages(), pltpu.VMEM((D, WIDE), bf16)],
        scratch_shapes=[
            pltpu.VMEM((TILE, WIDE), f32),
            pltpu.SemaphoreType.DMA((D // CHUNK,)),
        ],
        compiler_params=params(24),
        cost_estimate=LITTLE,
        name="gate",
    )(place, ratios, tokens, weight, hidden, up)


def terms(kinds, place, grad, weight, after=()):
    def body(place_ref, grad_ref, weight_ref, *refs):
        outs = refs[len(after) :]
        for i, kind in enumerate(kinds):
            put_terms(kind, place_ref, grad_ref, weight_ref, outs[2 * i : 2 * i + 2])

    return pl.pallas_call(
        body,
        in_specs=[SM, VM, VM] + [ANY] * len(after),
        out_specs=[VM] * 2 * len(kinds),
        out_shape=messages() * len(kinds),
        compiler_params=params(16),
        cost_estimate=LITTLE,
        name="terms",
    )(place, grad, weight, *after)


def add(a, b, after=()):
    return pl.pallas_call(
        skipping(add_body, 2, len(after)),
        in_specs=[VM, VM] + [ANY] * len(after),
        out_specs=VM,
        out_shape=jax.ShapeDtypeStruct(a.shape, bf16),
        compiler_params=params(6),
        cost_estimate=LITTLE,
        name="add",
    )(a, b, *after)


def own_body(axis, place_ref, a_ref, b_ref, c_ref, here, other_way, this_way, far):
    me, core = place_ref[1 if axis == "x" else 0], place_ref[2]
    for d, out_ref in ((0, here), (3 - 2 * core, other_way), (1 + 2 * core, this_way), (2, far)):
        j = lax.rem(me + d, SIDE)
        out_ref[...] = (
            a_ref[j].astype(f32) + b_ref[j].astype(f32) + c_ref[j].astype(f32)
        ).astype(bf16)


def own(axis, place, a, b, c, after=()):
    n = a.shape[1]
    return pl.pallas_call(
        skipping(functools.partial(own_body, axis), 4, len(after)),
        in_specs=[SM] + [VM] * 3 + [ANY] * len(after),
        out_specs=[VM] * SIDE,
        out_shape=[jax.ShapeDtypeStruct((n, OUT), bf16)] * SIDE,
        compiler_params=params(8),
        cost_estimate=LITTLE,
        name="own_" + axis,
    )(place, a, b, c, *after)


def pack_body(a_ref, b_ref, out_ref):
    out_ref[0] = a_ref[...]
    out_ref[1] = b_ref[...]


def pack(a, b, after=()):
    return pl.pallas_call(
        skipping(pack_body, 2, len(after)),
        in_specs=[VM, VM] + [ANY] * len(after),
        out_specs=VM,
        out_shape=jax.ShapeDtypeStruct((2, *a.shape), bf16),
        compiler_params=params(4),
        cost_estimate=LITTLE,
        name="pack",
    )(a, b, *after)


def add_terms(*refs):
    out_ref = refs[-1]
    for g, (_, base, n) in enumerate(GROUPS):
        here, far, near, theirs = refs[4 * g : 4 * g + 4]
        parts = [r.astype(f32) for r in (here[...], far[...], near[0], theirs[1])]
        out_ref[base : base + n] = ((parts[0] + parts[1]) + (parts[2] + parts[3])).astype(bf16)


DEEP = 512
HALVES = 1
STEPS = D // DEEP // HALVES


def merge_body(token_ref, grad_ref, error_ref, q_ref, *refs):
    high_ref, low_ref, left_ref = refs[-3:]
    m = dot(token_ref[...], grad_ref[...], TN) + error_ref[0].astype(f32)
    high = m.astype(bf16)
    high_ref[...] = high
    low_ref[...] = (m - high.astype(f32)).astype(bf16)
    left_ref[...] = dot(q_ref[...].astype(bf16), high, NT).astype(bf16)


def merge(tokens, grad, error, q_t, before=(), after=()):
    at = STEPS if before else 0
    wide = pl.BlockSpec((DEEP, WIDE), lambda i: (at + i, 0))
    return pl.pallas_call(
        skipping(merge_body, 4 + len(before), len(after)),
        grid=(STEPS,),
        in_specs=[
            pl.BlockSpec((ROWS, DEEP), lambda i: (0, at + i)),
            VM,
            pl.BlockSpec((1, DEEP, WIDE), lambda i: (0, at + i, 0)),
            VM,
        ]
        + [ANY] * (len(before) + len(after)),
        out_specs=[wide, wide, pl.BlockSpec((R, DEEP), lambda i: (0, at + i))],
        out_shape=[
            jax.ShapeDtypeStruct((D, WIDE), bf16),
            jax.ShapeDtypeStruct((D, WIDE), bf16),
            jax.ShapeDtypeStruct((R, D), bf16),
        ],
        input_output_aliases={4 + k: k for k in range(len(before))},
        compiler_params=params(16),
        cost_estimate=LITTLE,
        name="merge",
    )(tokens, grad, error, q_t, *before, *after)


def pair_sum_body(core_ref, a_ref, b_ref, out_ref):
    s = a_ref[...].astype(f32) + b_ref[...].astype(f32)
    half = R // 2
    out_ref[...] = jnp.where(core_ref[2] == 0, s[:half], s[half:]).astype(bf16)


def add_body(a_ref, b_ref, out_ref):
    out_ref[...] = (a_ref[...].astype(f32) + b_ref[...].astype(f32)).astype(bf16)


def halves_joined(place_ref, mine, theirs):
    a, b = mine[...].astype(f32), theirs[...].astype(f32)
    first = place_ref[2] == 0
    return jnp.concatenate([jnp.where(first, a, b), jnp.where(first, b, a)], axis=0)


def to_core():
    return [(2 * z + c, 2 * z + 1 - c) for z in range(SIDE) for c in range(2)]


def swap(array):
    return lax.ppermute(array, "dp", to_core())


def from_chip(array, second):
    ws = (3, 2, 1, 0) if second else (1, 0, 3, 2)
    to = [(2 * z + c, 2 * w + c) for z, w in enumerate(ws) for c in range(2)]
    return lax.ppermute(array, "dp", to)


def pair_sum(place, local, after=()):
    return pl.pallas_call(
        skipping(pair_sum_body, 3, len(after)),
        in_specs=[SM, VM, VM] + [ANY] * len(after),
        out_specs=VM,
        out_shape=jax.ShapeDtypeStruct((R // 2, local.shape[1]), bf16),
        compiler_params=params(4),
        cost_estimate=LITTLE,
        name="pair_sum",
    )(place, local, swap(local), *after)


def ortho_body(place_ref, mine, theirs, out_ref):
    left = halves_joined(place_ref, mine, theirs) * 0.125
    gram = lax.dot_general(left, left, NT, precision=highest, preferred_element_type=f32)
    row_id = lax.broadcasted_iota(jnp.int32, (R, R), 0)
    col_id = lax.broadcasted_iota(jnp.int32, (R, R), 1)
    work = jnp.concatenate([gram, (row_id == col_id).astype(f32)], axis=1)
    row_ids = lax.broadcasted_iota(jnp.int32, (R, 2 * R), 0)
    for k in range(R):
        scale = lax.rsqrt(work[k : k + 1, k : k + 1])
        row = work[k : k + 1, :] * scale
        col = work[:, k : k + 1] * scale
        work = jnp.where(row_ids > k, work - col * row, jnp.where(row_ids == k, row, work))
    inverse = work[:, R:]
    out_ref[...] = lax.dot_general(
        inverse, left, NN, precision=highest, preferred_element_type=f32
    ).astype(bf16)


def ortho(place, mine, theirs, after=()):
    return pl.pallas_call(
        skipping(ortho_body, 3, len(after)),
        in_specs=[SM, VM, VM] + [ANY] * len(after),
        out_specs=VM,
        out_shape=jax.ShapeDtypeStruct((R, D), bf16),
        compiler_params=params(12),
        cost_estimate=LITTLE,
        name="ortho",
    )(place, mine, theirs, *after)


def right_body(left_ref, high_ref, out_ref, total_ref):
    i = pl.program_id(0)
    term = dot(left_ref[...], high_ref[...], NN)

    @pl.when(i == 0)
    def _():
        total_ref[...] = term

    @pl.when(i > 0)
    def _():
        total_ref[...] += term

    @pl.when(i == D // DEEP - 1)
    def _():
        out_ref[...] = total_ref[...].astype(bf16)


def right(left, high, after=()):
    return pl.pallas_call(
        skipping(right_body, 2, len(after)),
        grid=(D // DEEP,),
        in_specs=[
            pl.BlockSpec((R, DEEP), lambda i: (0, i)),
            pl.BlockSpec((DEEP, WIDE), lambda i: (i, 0)),
        ]
        + [ANY] * len(after),
        out_specs=pl.BlockSpec((R, WIDE), lambda i: (0, 0)),
        out_shape=jax.ShapeDtypeStruct((R, WIDE), bf16),
        scratch_shapes=[pltpu.VMEM((R, WIDE), f32)],
        compiler_params=params(8),
        cost_estimate=LITTLE,
        name="right",
    )(left, high, *after)


def error_body(left_ref, high_ref, low_ref, mine, theirs, q_ref, out_ref):
    q_next = (mine[...].astype(f32) + theirs[...].astype(f32)) * 0.125
    q_ref[...] = q_next
    approx = dot(left_ref[...], q_next.astype(bf16), TN)
    out_ref[0] = (
        (high_ref[...].astype(f32) - approx) + low_ref[...].astype(f32)
    ).astype(bf16)


def error(left, high, low, mine, theirs):
    wide = pl.BlockSpec((DEEP, WIDE), lambda i: (i, 0))
    return pl.pallas_call(
        error_body,
        grid=(D // DEEP,),
        in_specs=[pl.BlockSpec((R, DEEP), lambda i: (0, i)), wide, wide, VM, VM],
        out_specs=[VM, pl.BlockSpec((1, DEEP, WIDE), lambda i: (0, i, 0))],
        out_shape=[
            jax.ShapeDtypeStruct((R, WIDE), f32),
            jax.ShapeDtypeStruct((1, D, WIDE), bf16),
        ],
        compiler_params=params(14),
        cost_estimate=LITTLE,
        name="error",
    )(left, high, low, mine, theirs)


def shards(tokens, gate_weight, up_values, hidden_grad, log_ratios, q_factors, error_feedback):
    spot = lax.axis_index("tensor").astype(jnp.int32)
    core = lax.axis_index("dp").astype(jnp.int32) & 1
    place = jnp.stack([spot & 3, spot >> 2, core])

    def along(axis, y, x, d):
        return ((y + d) % SIDE) * SIDE + x if axis == "y" else y * SIDE + (x + d) % SIDE

    spots = [(y, x) for y in range(SIDE) for x in range(SIDE)]
    n_spots = SIDE * SIDE

    def send(array, axis, d):
        to = [(y * SIDE + x, along(axis, y, x, d)) for y, x in spots]
        return lax.ppermute(array, "tensor", to)

    def send_on(array, axis):
        to = [
            (n_spots * i + y * SIDE + x, n_spots * i + along(axis, y, x, 1 + 2 * (i % 2)))
            for i in range(2 * SIDE)
            for y, x in spots
        ]
        return lax.ppermute(array, ("dp", "tensor"), to)

    in_hbm = lambda array: pltpu.with_memory_space_constraint(array, pltpu.HBM)
    tokens, up_values, hidden_grad, error_feedback = map(
        in_hbm, (tokens, up_values, hidden_grad, error_feedback)
    )
    q_t = q_factors.T

    grad, far_x, far_y, weight = gate(
        place, log_ratios.T, tokens, in_hbm(gate_weight), hidden_grad, up_values
    )
    far_x, far_y = send_on(far_x, "x"), send_on(far_y, "y")
    swapped = swap(grad)
    mine_x, mine_y, own_x, own_y = terms((NEAR, OWN), place, grad, weight)
    near_x, near_y = terms((NEAR,), place, swapped, weight, (mine_x,))
    m = near_x
    near_x, near_y = send_on(near_x, "x"), send_on(near_y, "y")
    high, low, left_local = merge(tokens, grad, error_feedback, q_t, after=(m,))
    message_x = add(mine_x, far_x, (left_local,))
    message_y = add(mine_y, far_y, (message_x,))
    last_x, last_y = send_on(message_x, "x"), send_on(message_y, "y")
    part = pair_sum(place, left_local, (message_y,))
    near_x, near_y, part = lax.optimization_barrier((near_x, near_y, part))
    near_x, near_y = swap(near_x), swap(near_y)
    part = add(part, from_chip(part, False))
    part = add(part, from_chip(part, True))

    def across(axis):
        return "y" if axis == "x" else "x"

    here_x, other_x, this_x, far_x = own("x", place, own_x, last_x, near_x, (part,))
    far_x, other_x = send(far_x, across("x"), 2), swap(other_x)
    here_y, other_y, this_y, far_y = own("y", place, own_y, last_y, near_y, (here_x,))
    far_y, other_y = send(far_y, across("y"), 2), swap(other_y)
    left = ortho(place, part, swap(part), (here_y,))
    right_local = right(left, high, (far_x, far_y))
    part = from_chip(right_local, False)
    next_x = send_on(pack(this_x, other_x, (right_local,)), across("x"))
    next_y = send_on(pack(this_y, other_y, (right_local,)), across("y"))
    part = add(right_local, part)
    part = add(part, from_chip(part, True))
    next_x, next_y, part = lax.optimization_barrier((next_x, next_y, part))
    q_next, error_next = error(left, high, low, part, swap(part))
    across_x = (here_x, far_x, next_x, swap(next_x))
    across_y = (here_y, far_y, next_y, swap(next_y))
    token_grad = pl.pallas_call(
        add_terms,
        in_specs=[VM] * 8,
        out_specs=VM,
        out_shape=jax.ShapeDtypeStruct((ROWS, OUT), bf16),
        compiler_params=params(8),
        cost_estimate=LITTLE,
        name="add_terms",
    )(*across_x, *across_y)
    return (token_grad, q_next.T, error_next)


def solution(mesh):
    return jax.shard_map(
        shards,
        mesh=mesh,
        in_specs=(
            P("dp", None),
            P(None, "tensor"),
            P("dp", "tensor"),
            P("dp", "tensor"),
            P("dp", None),
            P("tensor", None),
            P("dp", None, "tensor"),
        ),
        out_specs=(P("dp", "tensor"), P("tensor", None), P("dp", None, "tensor")),
        check_vma=False,
    )
```

time: 205 us -> 115 us (0.56); the launches traced: 203 us -> 115 us
  matrix products: 86.2 us -> 0 us
  Pallas kernels: 0 us -> 63.6 us
  starting transfers between devices: 0.26 us -> 33 us
  local copies, waits for them, and re-layouts: 27.1 us -> 0.69 us
  blocking collectives: 25.1 us -> 0 us
  waiting for transfers between devices: 41.3 us -> 16.9 us
  between operations: 15.5 us -> 0.84 us
  other arithmetic: 7.48 us -> 0.08 us
    dot_general x7 -> x0, matrix products: 84.6 us -> none  [the longest x1 20.5 us: shards(): lax.dot_general(gate_grad, gate_weight, (((1,), (1,)), ((), ())), preferr...]
    pallas_call x0 -> x19, Pallas kernels: none -> 63.6 us  [the longest x1 19.4 us: gate(): pl.pallas_call(gate_body, grid=(ROWS // TILE,), in_specs=[SM, SM, rows(D)...]
    psum x1 -> x0, waiting for transfers between devices: 41.2 us -> none  [shards(): lax.psum(left_local.astype(jnp.bfloat16), 'dp').astype(jnp.float32)]
    ppermute x0 -> x24, starting transfers between devices: none -> 33 us  [the longest x8 13.6 us: send_on(): return lax.ppermute(array, ('dp', 'tensor'), to)]
    unnamed x10 -> x4, local copies, waits for them, and re-layouts: 26.8 us -> 0.69 us
    psum x1 -> x0, blocking collectives: 25.1 us -> none  [shards(): lax.psum(right_local.astype(jnp.bfloat16), 'dp').astype(jnp.float32)]
    ppermute x0 -> x24, waiting for transfers between devices: none -> 16.9 us  [the longest x4 10.2 us: from_chip(): return lax.ppermute(array, 'dp', to)]
    another operation x6 -> x1, other arithmetic: 6.69 us -> 0.08 us  [shards(): place = jnp.stack([spot & 3, spot >> 2, core])]
  transfers between devices with their start and end apart: 2 -> 24, of which waited for: 1 -> 8; matrix products, arithmetic and copies ran while one was open for 31% -> 0% of each run, Pallas kernels for 0% -> 37%
where the time goes in v1:
time: 115 us
  Pallas kernels  63.6 us (55%)
  starting transfers between devices  33 us (29%)
  waiting for transfers between devices  16.9 us (15%)
    pallas_call x1, Pallas kernels, gate(): pl.pallas_call(gate_body, grid=(ROWS // TILE,), in_specs=[SM, SM, rows(D)...  19.4 us
    pallas_call x1, Pallas kernels, merge(): pl.pallas_call(skipping(merge_body, 4 + len(before), len(after)), grid=(S...  16.2 us
    ppermute x8, starting transfers between devices, send_on(): return lax.ppermute(array, ('dp', 'tensor'), to)  13.6 us
    ppermute x4, starting transfers between devices, from_chip(): return lax.ppermute(array, 'dp', to)  10.2 us
    ppermute x4, waiting for transfers between devices, from_chip(): return lax.ppermute(array, 'dp', to)  10.2 us
    pallas_call x2, Pallas kernels, terms(): pl.pallas_call(body, in_specs=[SM, VM, VM] + [ANY] * len(after), out_spec...  9.62 us
    pallas_call x1, Pallas kernels, error(): pl.pallas_call(error_body, grid=(D // DEEP,), in_specs=[pl.BlockSpec((R,...  6.22 us
    ppermute x10, starting transfers between devices, swap(): return lax.ppermute(array, 'dp', to_core())  5.69 us
  transfers between devices with their start and end apart: 24, of which 8 were waited for; matrix products, arithmetic and copies ran while one was open for 0% of the time, Pallas kernels for 37%

profile of v1, /device:TPU:1, one launch (start us, length us, event | category | flops | bytes accessed | tf_op | source)
XLA Modules:
  0.0 115.1 jit_solution(14681979465669754550)
XLA Ops:
  0.6 0.1 pad_add_fusion.place_ref.refs_0_
  0.7 0.7 copy-done.1
  1.4 19.4 %gate.1 = (bf16[1280,896]{1,0:T(8,128)(2,1)S(1)}, bf16[4,640,256]{2,1,0:T(8,128)(2,1)S(1)}, bf16[4,640,256]{2,1,0:T(8,128)(2,1)S(1)}, bf16[4096,896]{1,0:T(8,128)(2,1)S(1)}) custom-call(s32[3]{0:T(128)S(1)} %pad_add_fusion.place_ref.refs_0_, f32[2,8]{1,0:T(2,128)S(1)} %bitcast.7, bf16[1280,4096]{1,0:T(8,128)(2,1)} %refs_0_.1, bf16[4096,896]{1,0:T(8,128)(2,1)} %weight_hbm.1, ...), custom_call_target="tpu_custom_call" | custom-call | flops 1 | bytes 1 | tf_op jit(solution)/shard_map/gate/pallas_call | solution.py:142
  20.8 1.5 %collective-permute-start.1 = (bf16[1280,896]{1,0:T(8,128)(2,1)S(1)}, bf16[1280,896]{1,0:T(8,128)(2,1)S(1)}, u32[]{:S(2)}, u32[]{:S(2)}) collective-permute-start(bf16[1280,896]{1,0:T(8,128)(2,1)S(1)} %get-tuple-element.32.grad_ref.refs_1_), channel_id=1, source_target_pairs={{0,16},{16,0},{32,48},{48,32},{64,80},{80,64},{96,112},{112,96},{1... | collective-permute-start | bytes 6881288 | tf_op jit(solution)/shard_map/ppermute | solution.py:295
  22.3 2.6 %collective-permute-start = (bf16[4,640,256]{2,1,0:T(8,128)(2,1)S(1)}, bf16[4,640,256]{2,1,0:T(8,128)(2,1)S(1)}, u32[]{:S(2)}, u32[]{:S(2)}) collective-permute-start(bf16[4,640,256]{2,1,0:T(8,128)(2,1)S(1)} %get-tuple-element.36), channel_id=1, source_target_pairs={{0,1},{1,2},{2,3},{3,0},{4,5},{5,6},{6,7},{7,4},{8,9},{9,10},{10,1... | collective-permute-start | bytes 3932168 | tf_op jit(solution)/shard_map/ppermute | solution.py:428
  24.9 2.7 %collective-permute-start.6 = (bf16[4,640,256]{2,1,0:T(8,128)(2,1)S(1)}, bf16[4,640,256]{2,1,0:T(8,128)(2,1)S(1)}, u32[]{:S(2)}, u32[]{:S(2)}) collective-permute-start(bf16[4,640,256]{2,1,0:T(8,128)(2,1)S(1)} %get-tuple-element.41), channel_id=1, source_target_pairs={{0,4},{1,5},{2,6},{3,7},{4,8},{5,9},{6,10},{7,11},{8,12},{9,13},{1... | collective-permute-start | bytes 3932168 | tf_op jit(solution)/shard_map/ppermute | solution.py:428
  27.6 6.2 %terms.2 = (bf16[4,640,256]{2,1,0:T(8,128)(2,1)S(1)}, bf16[4,640,256]{2,1,0:T(8,128)(2,1)S(1)}, bf16[4,640,256]{2,1,0:T(8,128)(2,1)S(1)}, bf16[4,640,256]{2,1,0:T(8,128)(2,1)S(1)}) custom-call(s32[3]{0:T(128)S(1)} %pad_add_fusion.place_ref.refs_0_, bf16[1280,896]{1,0:T(8,128)(2,1)S(1)} %get-tuple-element.32.grad_ref.refs_1_, ...), custom_call_target="tpu_custom_call" | custom-call | flops 1 | bytes 1 | tf_op jit(solution)/shard_map/terms/pallas_call | solution.py:164
  33.8 0.0 collective-permute-done.1.grad_ref
  33.8 0.0 copy-start
  33.8 3.5 %terms.3 = (bf16[4,640,256]{2,1,0:T(8,128)(2,1)S(1)}, bf16[4,640,256]{2,1,0:T(8,128)(2,1)S(1)}) custom-call(s32[3]{0:T(128)S(1)} %pad_add_fusion.place_ref.refs_0_, bf16[1280,896]{1,0:T(8,128)(2,1)S(1)} %collective-permute-done.1.grad_ref, bf16[4096,896]{1,0:T(8,128)(2,1)S(1)} %get-tuple-element.33.weight_ref, bf16[4,640,256]{2,1,0:T(8,128)(2,1)S(1)} %get-tuple-element.35.refs_0_), custom_call_target="tpu_custom_call" | custom-call | flops 1 | bytes 1 | tf_op jit(solution)/shard_map/terms/pallas_call | solution.py:164
  37.3 0.6 collective-permute-start.3
  37.9 0.5 collective-permute-start.4
  38.3 16.2 %merge.1 = (bf16[4096,896]{1,0:T(8,128)(2,1)S(1)}, bf16[4096,896]{1,0:T(8,128)(2,1)S(1)}, bf16[32,4096]{1,0:T(8,128)(2,1)S(1)}) custom-call(bf16[1280,4096]{1,0:T(8,128)(2,1)} %refs_0_.1, bf16[1280,896]{1,0:T(8,128)(2,1)S(1)} %get-tuple-element.32.grad_ref.refs_1_, bf16[1,4096,896]{2,1,0:T(8,128)(2,1)} %refs_2_.1, f32[32,896]{1,0:T(8,128)S(1)} %bitcast.6, ...), custom_call_target="tpu_custom_call" | custom-call | flops 1 | bytes 1 | tf_op jit(solution)/shard_map/merge/pallas_call | solution.py:251
  54.5 0.1 collective-permute-start.5
  54.6 0.0 collective-permute-done.refs_1_
  54.6 0.3 add.10.refs_2_
  54.9 1.5 %collective-permute-start.2 = (bf16[4,640,256]{2,1,0:T(8,128)(2,1)S(1)}, bf16[4,640,256]{2,1,0:T(8,128)(2,1)S(1)}, u32[]{:S(2)}, u32[]{:S(2)}) collective-permute-start(bf16[4,640,256]{2,1,0:T(8,128)(2,1)S(1)} %add.10.refs_2_), channel_id=1, source_target_pairs={{0,1},{1,2},{2,3},{3,0},{4,5},{5,6},{6,7},{7,4},{8,9},{9,10},{10,1... | collective-permute-start | bytes 3932168 | tf_op jit(solution)/shard_map/ppermute | solution.py:428
  56.4 0.0 collective-permute-done.6.refs_1_
  56.4 0.3 add.11.refs_3_
  56.8 0.0 collective-permute-done.5.refs_2_
  56.8 0.6 pair_sum.1.refs_0_
  57.4 0.0 collective-permute-done.3
  57.4 0.0 collective-permute-done.4
  57.4 0.3 collective-permute-start.7
  57.8 1.6 %collective-permute-start.13 = (bf16[4,640,256]{2,1,0:T(8,128)(2,1)S(1)}, bf16[4,640,256]{2,1,0:T(8,128)(2,1)S(1)}, u32[]{:S(2)}, u32[]{:S(2)}) collective-permute-start(bf16[4,640,256]{2,1,0:T(8,128)(2,1)S(1)} %add.11.refs_3_), channel_id=1, source_target_pairs={{0,4},{1,5},{2,6},{3,7},{4,8},{5,9},{6,10},{7,11},{8,12},{9,13},{1... | collective-permute-start | bytes 3932168 | tf_op jit(solution)/shard_map/ppermute | solution.py:428
  59.3 0.0 collective-permute-start.14
  59.3 1.6 %collective-permute-start.8 = (bf16[16,4096]{1,0:T(8,128)(2,1)S(1)}, bf16[16,4096]{1,0:T(8,128)(2,1)S(1)}, u32[]{:S(2)}, u32[]{:S(2)}) collective-permute-start(bf16[16,4096]{1,0:T(8,128)(2,1)S(1)} %pair_sum.1.refs_0_), channel_id=1, source_target_pairs={{0,32},{16,48},{32,0},{48,16},{64,96},{80,112},{96,64},{112,80},{1... | collective-permute-start | bytes 393224 | tf_op jit(solution)/shard_map/ppermute | solution.py:301
  61.0 3.3 %collective-permute-done.8.refs_1_ = bf16[16,4096]{1,0:T(8,128)(2,1)S(1)} collective-permute-done((bf16[16,4096]{1,0:T(8,128)(2,1)S(1)}, bf16[16,4096]{1,0:T(8,128)(2,1)S(1)}, u32[]{:S(2)}, u32[]{:S(2)}) %collective-permute-start.8) | collective-permute-done | bytes 131104 | tf_op jit(solution)/shard_map/ppermute | solution.py:301
  64.3 3.5 %collective-permute-start.9 = (bf16[16,4096]{1,0:T(8,128)(2,1)S(1)}, bf16[16,4096]{1,0:T(8,128)(2,1)S(1)}, u32[]{:S(2)}, u32[]{:S(2)}) collective-permute-start(bf16[16,4096]{1,0:T(8,128)(2,1)S(1)} %add.12.refs_0_), channel_id=1, source_target_pairs={{0,96},{16,112},{32,64},{48,80},{64,32},{80,48},{96,0},{112,16},{1... | collective-permute-start | bytes 393224 | tf_op jit(solution)/shard_map/ppermute | solution.py:301
  67.7 2.7 %collective-permute-done.9.refs_1_ = bf16[16,4096]{1,0:T(8,128)(2,1)S(1)} collective-permute-done((bf16[16,4096]{1,0:T(8,128)(2,1)S(1)}, bf16[16,4096]{1,0:T(8,128)(2,1)S(1)}, u32[]{:S(2)}, u32[]{:S(2)}) %collective-permute-start.9) | collective-permute-done | bytes 131104 | tf_op jit(solution)/shard_map/ppermute | solution.py:301
  70.4 1.3 %collective-permute-done.2.refs_2_ = bf16[4,640,256]{2,1,0:T(8,128)(2,1)S(1)} collective-permute-done((bf16[4,640,256]{2,1,0:T(8,128)(2,1)S(1)}, bf16[4,640,256]{2,1,0:T(8,128)(2,1)S(1)}, u32[]{:S(2)}, u32[]{:S(2)}) %collective-permute-start.2) | collective-permute-done | bytes 1310752 | tf_op jit(solution)/shard_map/ppermute | solution.py:428
  71.8 0.0 collective-permute-done.7.refs_3_
  71.8 1.1 own_x.1
  72.8 1.7 %collective-permute-done.13.refs_2_ = bf16[4,640,256]{2,1,0:T(8,128)(2,1)S(1)} collective-permute-done((bf16[4,640,256]{2,1,0:T(8,128)(2,1)S(1)}, bf16[4,640,256]{2,1,0:T(8,128)(2,1)S(1)}, u32[]{:S(2)}, u32[]{:S(2)}) %collective-permute-start.13) | collective-permute-done | bytes 1310752 | tf_op jit(solution)/shard_map/ppermute | solution.py:428
  74.5 0.0 collective-permute-done.14.refs_3_
  74.5 1.0 own_y.1
  75.5 1.8 %collective-permute-start.15 = (bf16[640,256]{1,0:T(8,128)(2,1)S(1)}, bf16[640,256]{1,0:T(8,128)(2,1)S(1)}, u32[]{:S(2)}, u32[]{:S(2)}) collective-permute-start(bf16[640,256]{1,0:T(8,128)(2,1)S(1)} %get-tuple-element.52), channel_id=1, source_target_pairs={{0,2},{1,3},{2,0},{3,1},{4,6},{5,7},{6,4},{7,5},{8,10},{9,11},{10,... | collective-permute-start | bytes 983048 | tf_op jit(solution)/shard_map/ppermute | solution.py:420
  77.4 1.7 %collective-permute-start.10 = (bf16[640,256]{1,0:T(8,128)(2,1)S(1)}, bf16[640,256]{1,0:T(8,128)(2,1)S(1)}, u32[]{:S(2)}, u32[]{:S(2)}) collective-permute-start(bf16[640,256]{1,0:T(8,128)(2,1)S(1)} %get-tuple-element.45), channel_id=1, source_target_pairs={{0,8},{1,9},{2,10},{3,11},{4,12},{5,13},{6,14},{7,15},{8,0},{9,1},... | collective-permute-start | bytes 983048 | tf_op jit(solution)/shard_map/ppermute | solution.py:420
  79.1 1.4 %collective-permute-start.17 = (bf16[640,256]{1,0:T(8,128)(2,1)S(1)}, bf16[640,256]{1,0:T(8,128)(2,1)S(1)}, u32[]{:S(2)}, u32[]{:S(2)}) collective-permute-start(bf16[640,256]{1,0:T(8,128)(2,1)S(1)} %get-tuple-element.54), channel_id=1, source_target_pairs={{0,16},{16,0},{32,48},{48,32},{64,80},{80,64},{96,112},{112,96},{1... | collective-permute-start | bytes 983048 | tf_op jit(solution)/shard_map/ppermute | solution.py:295
  80.5 0.0 collective-permute-start.11
  80.5 0.5 collective-permute-start.12
  81.0 1.4 %collective-permute-done.12.refs_2_ = bf16[16,4096]{1,0:T(8,128)(2,1)S(1)} collective-permute-done((bf16[16,4096]{1,0:T(8,128)(2,1)S(1)}, bf16[16,4096]{1,0:T(8,128)(2,1)S(1)}, u32[]{:S(2)}, u32[]{:S(2)}) %collective-permute-start.12) | collective-permute-done | bytes 131104 | tf_op jit(solution)/shard_map/ppermute | solution.py:295
  82.4 5.1 %ortho.1.refs_0_.left_ref = bf16[32,4096]{1,0:T(8,128)(2,1)S(1)} custom-call(s32[3]{0:T(128)S(1)} %pad_add_fusion.place_ref.refs_0_, bf16[16,4096]{1,0:T(8,128)(2,1)S(1)} %add.13.refs_4_.refs_1_, bf16[16,4096]{1,0:T(8,128)(2,1)S(1)} %collective-permute-done.12.refs_2_, bf16[640,256]{1,0:T(8,128)(2,1)S(1)} %get-tuple-element.50.refs_3_.refs_4_), custom_call_target="tpu_custom_call" | custom-call | flops 1 | bytes 1 | tf_op jit(solution)/shard_map/ortho/pallas_call | solution.py:335
  87.5 0.0 collective-permute-done.15.refs_3_.refs_5_
  87.5 0.0 collective-permute-done.10.refs_2_.refs_1_
  87.5 2.5 %right.1.refs_2_.refs_0_ = bf16[32,896]{1,0:T(8,128)(2,1)S(1)} custom-call(bf16[32,4096]{1,0:T(8,128)(2,1)S(1)} %ortho.1.refs_0_.left_ref, bf16[4096,896]{1,0:T(8,128)(2,1)S(1)} %get-tuple-element.51.refs_1_.high_ref, bf16[640,256]{1,0:T(8,128)(2,1)S(1)} %collective-permute-done.10.refs_2_.refs_1_, bf16[640,256]{1,0:T(8,128)(2,1)S(1)} %collective-permute-done.15.refs_3_.refs_5_), custom_call_target="tpu_custom_call" | custom-call | flops 1 | bytes 1 | tf_op jit(solution)/shard_map/right/pallas_call | solution.py:364
  90.0 0.0 collective-permute-done.17.refs_1_
  90.0 1.2 %collective-permute-start.18 = (bf16[2,640,256]{2,1,0:T(8,128)(2,1)S(1)}, bf16[2,640,256]{2,1,0:T(8,128)(2,1)S(1)}, u32[]{:S(2)}, u32[]{:S(2)}) collective-permute-start(bf16[2,640,256]{2,1,0:T(8,128)(2,1)S(1)} %pack.3), channel_id=1, source_target_pairs={{0,1},{1,2},{2,3},{3,0},{4,5},{5,6},{6,7},{7,4},{8,9},{9,10},{10,1... | collective-permute-start | bytes 1966088 | tf_op jit(solution)/shard_map/ppermute | solution.py:428
  91.3 0.0 collective-permute-done.11.refs_1_
  91.3 3.0 %collective-permute-start.16 = (bf16[2,640,256]{2,1,0:T(8,128)(2,1)S(1)}, bf16[2,640,256]{2,1,0:T(8,128)(2,1)S(1)}, u32[]{:S(2)}, u32[]{:S(2)}) collective-permute-start(bf16[2,640,256]{2,1,0:T(8,128)(2,1)S(1)} %pack.2), channel_id=1, source_target_pairs={{0,4},{1,5},{2,6},{3,7},{4,8},{5,9},{6,10},{7,11},{8,12},{9,13},{1... | collective-permute-start | bytes 1966088 | tf_op jit(solution)/shard_map/ppermute | solution.py:428
  94.3 1.6 %collective-permute-start.19 = (bf16[32,896]{1,0:T(8,128)(2,1)S(1)}, bf16[32,896]{1,0:T(8,128)(2,1)S(1)}, u32[]{:S(2)}, u32[]{:S(2)}) collective-permute-start(bf16[32,896]{1,0:T(8,128)(2,1)S(1)} %right.1.refs_2_.refs_0_), channel_id=1, source_target_pairs={{0,32},{16,48},{32,0},{48,16},{64,96},{80,112},{96,64},{112,80},{1... | collective-permute-start | bytes 172040 | tf_op jit(solution)/shard_map/ppermute | solution.py:301
  95.9 2.4 %collective-permute-done.19.refs_1_ = bf16[32,896]{1,0:T(8,128)(2,1)S(1)} collective-permute-done((bf16[32,896]{1,0:T(8,128)(2,1)S(1)}, bf16[32,896]{1,0:T(8,128)(2,1)S(1)}, u32[]{:S(2)}, u32[]{:S(2)}) %collective-permute-start.19) | collective-permute-done | bytes 57376 | tf_op jit(solution)/shard_map/ppermute | solution.py:301
  98.3 3.5 %collective-permute-start.20 = (bf16[32,896]{1,0:T(8,128)(2,1)S(1)}, bf16[32,896]{1,0:T(8,128)(2,1)S(1)}, u32[]{:S(2)}, u32[]{:S(2)}) collective-permute-start(bf16[32,896]{1,0:T(8,128)(2,1)S(1)} %add.14.refs_0_), channel_id=1, source_target_pairs={{0,96},{16,112},{32,64},{48,80},{64,32},{80,48},{96,0},{112,16},{1... | collective-permute-start | bytes 172040 | tf_op jit(solution)/shard_map/ppermute | solution.py:301
  101.8 1.9 %collective-permute-done.20.refs_1_ = bf16[32,896]{1,0:T(8,128)(2,1)S(1)} collective-permute-done((bf16[32,896]{1,0:T(8,128)(2,1)S(1)}, bf16[32,896]{1,0:T(8,128)(2,1)S(1)}, u32[]{:S(2)}, u32[]{:S(2)}) %collective-permute-start.20) | collective-permute-done | bytes 57376 | tf_op jit(solution)/shard_map/ppermute | solution.py:301
  103.6 0.0 collective-permute-done.18.refs_6_
  103.7 0.0 collective-permute-done.16.refs_2_
  103.7 1.3 %collective-permute-start.21 = (bf16[2,640,256]{2,1,0:T(8,128)(2,1)S(1)}, bf16[2,640,256]{2,1,0:T(8,128)(2,1)S(1)}, u32[]{:S(2)}, u32[]{:S(2)}) collective-permute-start(bf16[2,640,256]{2,1,0:T(8,128)(2,1)S(1)} %collective-permute-done.16.refs_2_), channel_id=1, source_target_pairs={{0,16},{16,0},{32,48},{48,32},{64,80},{80,64},{96,112},{112,96},{1... | collective-permute-start | bytes 1966088 | tf_op jit(solution)/shard_map/ppermute | solution.py:295
  105.0 0.1 collective-permute-start.22
  105.1 0.4 collective-permute-start.23
  105.5 2.2 %collective-permute-done.23.theirs = bf16[32,896]{1,0:T(8,128)(2,1)S(1)} collective-permute-done((bf16[32,896]{1,0:T(8,128)(2,1)S(1)}, bf16[32,896]{1,0:T(8,128)(2,1)S(1)}, u32[]{:S(2)}, u32[]{:S(2)}) %collective-permute-start.23) | collective-permute-done | bytes 57376 | tf_op jit(solution)/shard_map/ppermute | solution.py:295
  107.7 6.2 %error.1 = (f32[32,896]{1,0:T(8,128)}, bf16[1,4096,896]{2,1,0:T(8,128)(2,1)}) custom-call(bf16[32,4096]{1,0:T(8,128)(2,1)S(1)} %ortho.1.refs_0_.left_ref, bf16[4096,896]{1,0:T(8,128)(2,1)S(1)} %get-tuple-element.51.refs_1_.high_ref, bf16[4096,896]{1,0:T(8,128)(2,1)S(1)} %get-tuple-element.57.low_ref, bf16[32,896]{1,0:T(8,128)(2,1)S(1)} %add.15.mine, ...), custom_call_target="tpu_custom_call" | custom-call | flops 1 | bytes 1 | tf_op jit(solution)/shard_map/error/pallas_call | solution.py:392
  114.0 0.0 collective-permute-done.21.refs_3_
  114.0 0.0 collective-permute-done.22.refs_7_
  114.0 1.2 %add_terms.1 = bf16[1280,256]{1,0:T(8,128)(2,1)} custom-call(bf16[640,256]{1,0:T(8,128)(2,1)S(1)} %get-tuple-element.44.refs_4_.refs_0_, bf16[640,256]{1,0:T(8,128)(2,1)S(1)} %collective-permute-done.10.refs_2_.refs_1_, bf16[2,640,256]{2,1,0:T(8,128)(2,1)S(1)} %collective-permute-done.16.refs_2_, bf16[2,640,256]{2,1,0:T(8,128)(2,1)S(1)} %collective-permute-done.21.refs_3_, ...), custom_call_target="tpu_custom_call" | custom-call | flops 1 | bytes 1 | tf_op jit(solution)/shard_map/add_terms/pallas_call | solution.py:473
  (8 shorter events, 0.2 us)
Async XLA Ops:
  0.7 0.7 copy-start.1
  20.8 13.0 %collective-permute-start.1 = (bf16[1280,896]{1,0:T(8,128)(2,1)S(1)}, bf16[1280,896]{1,0:T(8,128)(2,1)S(1)}, u32[]{:S(2)}, u32[]{:S(2)}) collective-permute-start(bf16[1280,896]{1,0:T(8,128)(2,1)S(1)} %get-tuple-element.32.grad_ref.refs_1_), channel_id=1, source_target_pairs={{0,16},{16,0},{32,48},{48,32},{64,80},{80,64},{96,112},{112,96},{1... | collective-permute-start | bytes 6881288 | tf_op jit(solution)/shard_map/ppermute | solution.py:295
  22.3 32.3 %collective-permute-start = (bf16[4,640,256]{2,1,0:T(8,128)(2,1)S(1)}, bf16[4,640,256]{2,1,0:T(8,128)(2,1)S(1)}, u32[]{:S(2)}, u32[]{:S(2)}) collective-permute-start(bf16[4,640,256]{2,1,0:T(8,128)(2,1)S(1)} %get-tuple-element.36), channel_id=1, source_target_pairs={{0,1},{1,2},{2,3},{3,0},{4,5},{5,6},{6,7},{7,4},{8,9},{9,10},{10,1... | collective-permute-start | bytes 3932168 | tf_op jit(solution)/shard_map/ppermute | solution.py:428
  24.9 31.6 %collective-permute-start.6 = (bf16[4,640,256]{2,1,0:T(8,128)(2,1)S(1)}, bf16[4,640,256]{2,1,0:T(8,128)(2,1)S(1)}, u32[]{:S(2)}, u32[]{:S(2)}) collective-permute-start(bf16[4,640,256]{2,1,0:T(8,128)(2,1)S(1)} %get-tuple-element.41), channel_id=1, source_target_pairs={{0,4},{1,5},{2,6},{3,7},{4,8},{5,9},{6,10},{7,11},{8,12},{9,13},{1... | collective-permute-start | bytes 3932168 | tf_op jit(solution)/shard_map/ppermute | solution.py:428
  33.8 4.6 %copy-start = (f32[896,32]{0,1:T(8,128)S(1)}, f32[896,32]{0,1:T(8,128)}, u32[]{:S(2)}) copy-start(f32[896,32]{0,1:T(8,128)} %param.12) | copy-start | bytes 344068
  37.3 20.2 %collective-permute-start.3 = (bf16[4,640,256]{2,1,0:T(8,128)(2,1)S(1)}, bf16[4,640,256]{2,1,0:T(8,128)(2,1)S(1)}, u32[]{:S(2)}, u32[]{:S(2)}) collective-permute-start(bf16[4,640,256]{2,1,0:T(8,128)(2,1)S(1)} %get-tuple-element.37.refs_4_), channel_id=1, source_target_pairs={{0,1},{1,2},{2,3},{3,0},{4,5},{5,6},{6,7},{7,4},{8,9},{9,10},{10,1... | collective-permute-start | bytes 3932168 | tf_op jit(solution)/shard_map/ppermute | solution.py:428
  37.9 19.6 %collective-permute-start.4 = (bf16[4,640,256]{2,1,0:T(8,128)(2,1)S(1)}, bf16[4,640,256]{2,1,0:T(8,128)(2,1)S(1)}, u32[]{:S(2)}, u32[]{:S(2)}) collective-permute-start(bf16[4,640,256]{2,1,0:T(8,128)(2,1)S(1)} %get-tuple-element.39), channel_id=1, source_target_pairs={{0,4},{1,5},{2,6},{3,7},{4,8},{5,9},{6,10},{7,11},{8,12},{9,13},{1... | collective-permute-start | bytes 3932168 | tf_op jit(solution)/shard_map/ppermute | solution.py:428
  54.5 2.3 %collective-permute-start.5 = (bf16[32,4096]{1,0:T(8,128)(2,1)S(1)}, bf16[32,4096]{1,0:T(8,128)(2,1)S(1)}, u32[]{:S(2)}, u32[]{:S(2)}) collective-permute-start(bf16[32,4096]{1,0:T(8,128)(2,1)S(1)} %get-tuple-element.38.refs_2_.refs_1_), channel_id=1, source_target_pairs={{0,16},{16,0},{32,48},{48,32},{64,80},{80,64},{96,112},{112,96},{1... | collective-permute-start | bytes 786440 | tf_op jit(solution)/shard_map/ppermute | solution.py:295
  54.9 16.8 %collective-permute-start.2 = (bf16[4,640,256]{2,1,0:T(8,128)(2,1)S(1)}, bf16[4,640,256]{2,1,0:T(8,128)(2,1)S(1)}, u32[]{:S(2)}, u32[]{:S(2)}) collective-permute-start(bf16[4,640,256]{2,1,0:T(8,128)(2,1)S(1)} %add.10.refs_2_), channel_id=1, source_target_pairs={{0,1},{1,2},{2,3},{3,0},{4,5},{5,6},{6,7},{7,4},{8,9},{9,10},{10,1... | collective-permute-start | bytes 3932168 | tf_op jit(solution)/shard_map/ppermute | solution.py:428
  57.4 14.3 %collective-permute-start.7 = (bf16[4,640,256]{2,1,0:T(8,128)(2,1)S(1)}, bf16[4,640,256]{2,1,0:T(8,128)(2,1)S(1)}, u32[]{:S(2)}, u32[]{:S(2)}) collective-permute-start(bf16[4,640,256]{2,1,0:T(8,128)(2,1)S(1)} %collective-permute-done.3), channel_id=1, source_target_pairs={{0,16},{16,0},{32,48},{48,32},{64,80},{80,64},{96,112},{112,96},{1... | collective-permute-start | bytes 3932168 | tf_op jit(solution)/shard_map/ppermute | solution.py:295
  57.8 16.8 %collective-permute-start.13 = (bf16[4,640,256]{2,1,0:T(8,128)(2,1)S(1)}, bf16[4,640,256]{2,1,0:T(8,128)(2,1)S(1)}, u32[]{:S(2)}, u32[]{:S(2)}) collective-permute-start(bf16[4,640,256]{2,1,0:T(8,128)(2,1)S(1)} %add.11.refs_3_), channel_id=1, source_target_pairs={{0,4},{1,5},{2,6},{3,7},{4,8},{5,9},{6,10},{7,11},{8,12},{9,13},{1... | collective-permute-start | bytes 3932168 | tf_op jit(solution)/shard_map/ppermute | solution.py:428
  59.3 15.2 %collective-permute-start.14 = (bf16[4,640,256]{2,1,0:T(8,128)(2,1)S(1)}, bf16[4,640,256]{2,1,0:T(8,128)(2,1)S(1)}, u32[]{:S(2)}, u32[]{:S(2)}) collective-permute-start(bf16[4,640,256]{2,1,0:T(8,128)(2,1)S(1)} %collective-permute-done.4), channel_id=1, source_target_pairs={{0,16},{16,0},{32,48},{48,32},{64,80},{80,64},{96,112},{112,96},{1... | collective-permute-start | bytes 3932168 | tf_op jit(solution)/shard_map/ppermute | solution.py:295
  59.3 4.9 %collective-permute-start.8 = (bf16[16,4096]{1,0:T(8,128)(2,1)S(1)}, bf16[16,4096]{1,0:T(8,128)(2,1)S(1)}, u32[]{:S(2)}, u32[]{:S(2)}) collective-permute-start(bf16[16,4096]{1,0:T(8,128)(2,1)S(1)} %pair_sum.1.refs_0_), channel_id=1, source_target_pairs={{0,32},{16,48},{32,0},{48,16},{64,96},{80,112},{96,64},{112,80},{1... | collective-permute-start | bytes 393224 | tf_op jit(solution)/shard_map/ppermute | solution.py:301
  64.3 6.1 %collective-permute-start.9 = (bf16[16,4096]{1,0:T(8,128)(2,1)S(1)}, bf16[16,4096]{1,0:T(8,128)(2,1)S(1)}, u32[]{:S(2)}, u32[]{:S(2)}) collective-permute-start(bf16[16,4096]{1,0:T(8,128)(2,1)S(1)} %add.12.refs_0_), channel_id=1, source_target_pairs={{0,96},{16,112},{32,64},{48,80},{64,32},{80,48},{96,0},{112,16},{1... | collective-permute-start | bytes 393224 | tf_op jit(solution)/shard_map/ppermute | solution.py:301
  75.5 11.9 %collective-permute-start.15 = (bf16[640,256]{1,0:T(8,128)(2,1)S(1)}, bf16[640,256]{1,0:T(8,128)(2,1)S(1)}, u32[]{:S(2)}, u32[]{:S(2)}) collective-permute-start(bf16[640,256]{1,0:T(8,128)(2,1)S(1)} %get-tuple-element.52), channel_id=1, source_target_pairs={{0,2},{1,3},{2,0},{3,1},{4,6},{5,7},{6,4},{7,5},{8,10},{9,11},{10,... | collective-permute-start | bytes 983048 | tf_op jit(solution)/shard_map/ppermute | solution.py:420
  77.4 10.1 %collective-permute-start.10 = (bf16[640,256]{1,0:T(8,128)(2,1)S(1)}, bf16[640,256]{1,0:T(8,128)(2,1)S(1)}, u32[]{:S(2)}, u32[]{:S(2)}) collective-permute-start(bf16[640,256]{1,0:T(8,128)(2,1)S(1)} %get-tuple-element.45), channel_id=1, source_target_pairs={{0,8},{1,9},{2,10},{3,11},{4,12},{5,13},{6,14},{7,15},{8,0},{9,1},... | collective-permute-start | bytes 983048 | tf_op jit(solution)/shard_map/ppermute | solution.py:420
  79.1 10.9 %collective-permute-start.17 = (bf16[640,256]{1,0:T(8,128)(2,1)S(1)}, bf16[640,256]{1,0:T(8,128)(2,1)S(1)}, u32[]{:S(2)}, u32[]{:S(2)}) collective-permute-start(bf16[640,256]{1,0:T(8,128)(2,1)S(1)} %get-tuple-element.54), channel_id=1, source_target_pairs={{0,16},{16,0},{32,48},{48,32},{64,80},{80,64},{96,112},{112,96},{1... | collective-permute-start | bytes 983048 | tf_op jit(solution)/shard_map/ppermute | solution.py:295
  80.5 10.8 %collective-permute-start.11 = (bf16[640,256]{1,0:T(8,128)(2,1)S(1)}, bf16[640,256]{1,0:T(8,128)(2,1)S(1)}, u32[]{:S(2)}, u32[]{:S(2)}) collective-permute-start(bf16[640,256]{1,0:T(8,128)(2,1)S(1)} %get-tuple-element.47), channel_id=1, source_target_pairs={{0,16},{16,0},{32,48},{48,32},{64,80},{80,64},{96,112},{112,96},{1... | collective-permute-start | bytes 983048 | tf_op jit(solution)/shard_map/ppermute | solution.py:295
  80.5 1.9 %collective-permute-start.12 = (bf16[16,4096]{1,0:T(8,128)(2,1)S(1)}, bf16[16,4096]{1,0:T(8,128)(2,1)S(1)}, u32[]{:S(2)}, u32[]{:S(2)}) collective-permute-start(bf16[16,4096]{1,0:T(8,128)(2,1)S(1)} %add.13.refs_4_.refs_1_), channel_id=1, source_target_pairs={{0,16},{16,0},{32,48},{48,32},{64,80},{80,64},{96,112},{112,96},{1... | collective-permute-start | bytes 393224 | tf_op jit(solution)/shard_map/ppermute | solution.py:295
  90.0 13.6 %collective-permute-start.18 = (bf16[2,640,256]{2,1,0:T(8,128)(2,1)S(1)}, bf16[2,640,256]{2,1,0:T(8,128)(2,1)S(1)}, u32[]{:S(2)}, u32[]{:S(2)}) collective-permute-start(bf16[2,640,256]{2,1,0:T(8,128)(2,1)S(1)} %pack.3), channel_id=1, source_target_pairs={{0,1},{1,2},{2,3},{3,0},{4,5},{5,6},{6,7},{7,4},{8,9},{9,10},{10,1... | collective-permute-start | bytes 1966088 | tf_op jit(solution)/shard_map/ppermute | solution.py:428
  91.3 12.4 %collective-permute-start.16 = (bf16[2,640,256]{2,1,0:T(8,128)(2,1)S(1)}, bf16[2,640,256]{2,1,0:T(8,128)(2,1)S(1)}, u32[]{:S(2)}, u32[]{:S(2)}) collective-permute-start(bf16[2,640,256]{2,1,0:T(8,128)(2,1)S(1)} %pack.2), channel_id=1, source_target_pairs={{0,4},{1,5},{2,6},{3,7},{4,8},{5,9},{6,10},{7,11},{8,12},{9,13},{1... | collective-permute-start | bytes 1966088 | tf_op jit(solution)/shard_map/ppermute | solution.py:428
  94.3 4.0 %collective-permute-start.19 = (bf16[32,896]{1,0:T(8,128)(2,1)S(1)}, bf16[32,896]{1,0:T(8,128)(2,1)S(1)}, u32[]{:S(2)}, u32[]{:S(2)}) collective-permute-start(bf16[32,896]{1,0:T(8,128)(2,1)S(1)} %right.1.refs_2_.refs_0_), channel_id=1, source_target_pairs={{0,32},{16,48},{32,0},{48,16},{64,96},{80,112},{96,64},{112,80},{1... | collective-permute-start | bytes 172040 | tf_op jit(solution)/shard_map/ppermute | solution.py:301
  98.3 5.3 %collective-permute-start.20 = (bf16[32,896]{1,0:T(8,128)(2,1)S(1)}, bf16[32,896]{1,0:T(8,128)(2,1)S(1)}, u32[]{:S(2)}, u32[]{:S(2)}) collective-permute-start(bf16[32,896]{1,0:T(8,128)(2,1)S(1)} %add.14.refs_0_), channel_id=1, source_target_pairs={{0,96},{16,112},{32,64},{48,80},{64,32},{80,48},{96,0},{112,16},{1... | collective-permute-start | bytes 172040 | tf_op jit(solution)/shard_map/ppermute | solution.py:301
  103.7 10.3 %collective-permute-start.21 = (bf16[2,640,256]{2,1,0:T(8,128)(2,1)S(1)}, bf16[2,640,256]{2,1,0:T(8,128)(2,1)S(1)}, u32[]{:S(2)}, u32[]{:S(2)}) collective-permute-start(bf16[2,640,256]{2,1,0:T(8,128)(2,1)S(1)} %collective-permute-done.16.refs_2_), channel_id=1, source_target_pairs={{0,16},{16,0},{32,48},{48,32},{64,80},{80,64},{96,112},{112,96},{1... | collective-permute-start | bytes 1966088 | tf_op jit(solution)/shard_map/ppermute | solution.py:295
  105.0 9.0 %collective-permute-start.22 = (bf16[2,640,256]{2,1,0:T(8,128)(2,1)S(1)}, bf16[2,640,256]{2,1,0:T(8,128)(2,1)S(1)}, u32[]{:S(2)}, u32[]{:S(2)}) collective-permute-start(bf16[2,640,256]{2,1,0:T(8,128)(2,1)S(1)} %collective-permute-done.18.refs_6_), channel_id=1, source_target_pairs={{0,16},{16,0},{32,48},{48,32},{64,80},{80,64},{96,112},{112,96},{1... | collective-permute-start | bytes 1966088 | tf_op jit(solution)/shard_map/ppermute | solution.py:295
  105.1 2.7 %collective-permute-start.23 = (bf16[32,896]{1,0:T(8,128)(2,1)S(1)}, bf16[32,896]{1,0:T(8,128)(2,1)S(1)}, u32[]{:S(2)}, u32[]{:S(2)}) collective-permute-start(bf16[32,896]{1,0:T(8,128)(2,1)S(1)} %add.15.mine), channel_id=1, source_target_pairs={{0,16},{16,0},{32,48},{48,32},{64,80},{80,64},{96,112},{112,96},{1... | collective-permute-start | bytes 172040 | tf_op jit(solution)/shard_map/ppermute | solution.py:295

commit v2 on v1

--- a/solution.py
+++ b/solution.py
@@ -82,8 +82,8 @@
 
 
 def gate_grad_of(pair, ratio_ref, gate_pre, hidden, up):
-    margin = dpo_beta * (ratio_ref[0, pair] - ratio_ref[1, pair])
-    scaled = dpo_beta * jax.nn.sigmoid(jnp.full((PAIR, 1), -margin, f32))
+    margin = dpo_beta * (ratio_ref[0:1, :] - ratio_ref[1:2, :])
+    scaled = dpo_beta * jax.nn.sigmoid(-margin[:, pair : pair + 1])
     chosen = lax.broadcasted_iota(jnp.int32, (PAIR, 1), 0) < LEN
     row_weight = jnp.where(chosen, -scaled, scaled)
     s = jax.nn.sigmoid(gate_pre)
@@ -92,45 +92,62 @@
 
 
 def gate_body(
-    place_ref, ratio_ref, token_ref, weight_hbm, hidden_ref, up_ref,
-    grad_ref, far_x, far_y, weight_ref, pre_ref, sems,
+    place_ref, ratio_hbm, token_hbm, weight_hbm, hidden_hbm, up_hbm,
+    grad_ref, far_x, far_y, weight_ref, token_ref, hidden_ref, up_ref, ratio_ref, pre_ref, sems,
 ):
-    i = pl.program_id(0)
-
-    def chunk(k):
-        at = pl.ds(k * CHUNK, CHUNK)
-        return pltpu.make_async_copy(weight_hbm.at[at], weight_ref.at[at], sems.at[k])
-
-    def finish(gate_pre):
+    n_chunks, n_tiles = D // CHUNK, ROWS // TILE
+    chunks = [slice(k * CHUNK, (k + 1) * CHUNK) for k in range(n_chunks)]
+    tiles = [slice(t * TILE, (t + 1) * TILE) for t in range(n_tiles)]
+    pairs = [
+        (source.at[at], target.at[at])
+        for source, target, places in (
+            (weight_hbm, weight_ref, [(at,) for at in chunks]),
+            (token_hbm, token_ref, [(tiles[0], at) for at in chunks]),
+            (token_hbm, token_ref, [(at,) for at in tiles[1:]]),
+            (hidden_hbm, hidden_ref, [(at,) for at in tiles]),
+            (up_hbm, up_ref, [(at,) for at in tiles]),
+        )
+        for at in places
+    ]
+    copies = [pltpu.make_async_copy(*pair, sems.at[i]) for i, pair in enumerate(pairs)]
+    weights, first, copies = copies[:n_chunks], copies[n_chunks : 2 * n_chunks], copies[2 * n_chunks :]
+    later, hidden, up = copies[: n_tiles - 1], copies[n_tiles - 1 : 2 * n_tiles - 1], copies[2 * n_tiles - 1 :]
+    ratios = pltpu.make_async_copy(ratio_hbm, ratio_ref, sems.at[len(pairs)])
+    ratios.start()
+    for k in range(n_chunks):
+        weights[k].start()
+        first[k].start()
+    for t in range(n_tiles):
+        if t:
+            later[t - 1].start()
+        hidden[t].start()
+        up[t].start()
+
+
+    for t in range(n_tiles):
+        if t == 0:
+            for k, at in enumerate(chunks):
+                weights[k].wait()
+                first[k].wait()
+                part = dot(token_ref[tiles[0], at], weight_ref[at], NN)
+                if k == 0:
+                    pre_ref[...] = part
+                elif k < n_chunks - 1:
+                    pre_ref[...] += part
+            gate_pre = pre_ref[...] + part
+            ratios.wait()
+        else:
+            later[t - 1].wait()
+            gate_pre = dot(token_ref[tiles[t]], weight_ref[...], NN)
+        hidden[t].wait()
+        up[t].wait()
         for p in range(TILE // PAIR):
-            at = slice(p * PAIR, (p + 1) * PAIR)
-            row = pl.multiple_of(i * TILE + p * PAIR, PAIR)
-            grad_ref[pl.ds(row, PAIR)] = gate_grad_of(
-                i * (TILE // PAIR) + p, ratio_ref, gate_pre[at], hidden_ref[at], up_ref[at]
+            row = t * TILE + p * PAIR
+            at = slice(row, row + PAIR)
+            grad_ref[at] = gate_grad_of(
+                row // PAIR, ratio_ref, gate_pre[p * PAIR : (p + 1) * PAIR], hidden_ref[at], up_ref[at]
             )
-
-    @pl.when(i == 0)
-    def _():
-        for k in range(D // CHUNK):
-            chunk(k).start()
-        for k in range(D // CHUNK):
-            chunk(k).wait()
-            at = slice(k * CHUNK, (k + 1) * CHUNK)
-            part = dot(token_ref[:, at], weight_ref[at], NN)
-            if k == 0:
-                pre_ref[...] = part
-            elif k < D // CHUNK - 1:
-                pre_ref[...] += part
-            else:
-                finish(pre_ref[...] + part)
-
-    @pl.when(i > 0)
-    def _():
-        finish(dot(token_ref[...], weight_ref[...], NN))
-
-    @pl.when(i == ROWS // TILE - 1)
-    def _():
-        put_terms(FAR, place_ref, grad_ref, weight_ref, (far_x, far_y))
+    put_terms(FAR, place_ref, grad_ref, weight_ref, (far_x, far_y))
 
 
 def messages():
@@ -138,18 +155,20 @@
 
 
 def gate(place, ratios, tokens, weight, hidden, up):
-    rows = lambda wide: pl.BlockSpec((TILE, wide), lambda i: (i, 0))
     return pl.pallas_call(
         gate_body,
-        grid=(ROWS // TILE,),
-        in_specs=[SM, SM, rows(D), HBM, rows(WIDE), rows(WIDE)],
+        in_specs=[SM, HBM, HBM, HBM, HBM, HBM],
         out_specs=[VM] * 4,
         out_shape=[jax.ShapeDtypeStruct((ROWS, WIDE), bf16), *messages(), pltpu.VMEM((D, WIDE), bf16)],
         scratch_shapes=[
+            pltpu.VMEM((ROWS, D), bf16),
+            pltpu.VMEM((ROWS, WIDE), bf16),
+            pltpu.VMEM((ROWS, WIDE), bf16),
+            pltpu.VMEM((2, ROWS // PAIR), f32),
             pltpu.VMEM((TILE, WIDE), f32),
-            pltpu.SemaphoreType.DMA((D // CHUNK,)),
+            pltpu.SemaphoreType.DMA((2 * (D // CHUNK) + 3 * (ROWS // TILE),)),
         ],
-        compiler_params=params(24),
+        compiler_params=params(30),
         cost_estimate=LITTLE,
         name="gate",
     )(place, ratios, tokens, weight, hidden, up)
@@ -232,43 +251,38 @@
 
 
 DEEP = 512
-HALVES = 1
-STEPS = D // DEEP // HALVES
-
-
-def merge_body(token_ref, grad_ref, error_ref, q_ref, *refs):
-    high_ref, low_ref, left_ref = refs[-3:]
+
+
+def merge_body(token_ref, grad_ref, error_ref, q_ref, high_ref, low_ref, left_ref):
+    at = pl.ds(pl.multiple_of(pl.program_id(0) * DEEP, DEEP), DEEP)
     m = dot(token_ref[...], grad_ref[...], TN) + error_ref[0].astype(f32)
     high = m.astype(bf16)
-    high_ref[...] = high
-    low_ref[...] = (m - high.astype(f32)).astype(bf16)
+    high_ref[at] = high
+    low_ref[at] = (m - high.astype(f32)).astype(bf16)
     left_ref[...] = dot(q_ref[...].astype(bf16), high, NT).astype(bf16)
 
 
-def merge(tokens, grad, error, q_t, before=(), after=()):
-    at = STEPS if before else 0
-    wide = pl.BlockSpec((DEEP, WIDE), lambda i: (at + i, 0))
-    return pl.pallas_call(
-        skipping(merge_body, 4 + len(before), len(after)),
-        grid=(STEPS,),
+def merge(tokens, grad, error, q_t, after=()):
+    return pl.pallas_call(
+        skipping(merge_body, 4, len(after)),
+        grid=(D // DEEP,),
         in_specs=[
-            pl.BlockSpec((ROWS, DEEP), lambda i: (0, at + i)),
+            pl.BlockSpec((ROWS, DEEP), lambda i: (0, i)),
             VM,
-            pl.BlockSpec((1, DEEP, WIDE), lambda i: (0, at + i, 0)),
+            pl.BlockSpec((1, DEEP, WIDE), lambda i: (0, i, 0)),
             VM,
         ]
-        + [ANY] * (len(before) + len(after)),
-        out_specs=[wide, wide, pl.BlockSpec((R, DEEP), lambda i: (0, at + i))],
+        + [ANY] * len(after),
+        out_specs=[VM, VM, pl.BlockSpec((R, DEEP), lambda i: (0, i))],
         out_shape=[
-            jax.ShapeDtypeStruct((D, WIDE), bf16),
-            jax.ShapeDtypeStruct((D, WIDE), bf16),
+            pltpu.VMEM((D, WIDE), bf16),
+            pltpu.VMEM((D, WIDE), bf16),
             jax.ShapeDtypeStruct((R, D), bf16),
         ],
-        input_output_aliases={4 + k: k for k in range(len(before))},
-        compiler_params=params(16),
+        compiler_params=params(14),
         cost_estimate=LITTLE,
         name="merge",
-    )(tokens, grad, error, q_t, *before, *after)
+    )(tokens, grad, error, q_t, *after)
 
 
 def pair_sum_body(core_ref, a_ref, b_ref, out_ref):
@@ -295,12 +309,34 @@
     return lax.ppermute(array, "dp", to_core())
 
 
-def from_chip(array, second):
+def from_chip(array, d):
+    to = [(2 * z + c, 2 * ((z + d) % SIDE) + c) for z in range(SIDE) for c in range(2)]
+    return lax.ppermute(array, "dp", to)
+
+
+def from_neighbour(array, second):
     ws = (3, 2, 1, 0) if second else (1, 0, 3, 2)
     to = [(2 * z + c, 2 * w + c) for z, w in enumerate(ws) for c in range(2)]
     return lax.ppermute(array, "dp", to)
 
 
+def chips_sum_body(a_ref, b_ref, c_ref, d_ref, out_ref):
+    a, b, c, d = (r[...].astype(f32) for r in (a_ref, b_ref, c_ref, d_ref))
+    out_ref[...] = ((a + c) + (b + d)).astype(bf16)
+
+
+def chips_sum(arrays, after=()):
+    return pl.pallas_call(
+        skipping(chips_sum_body, SIDE, len(after)),
+        in_specs=[VM] * SIDE + [ANY] * len(after),
+        out_specs=VM,
+        out_shape=jax.ShapeDtypeStruct(arrays[0].shape, bf16),
+        compiler_params=params(4),
+        cost_estimate=LITTLE,
+        name="chips_sum",
+    )(*arrays, *after)
+
+
 def pair_sum(place, local, after=()):
     return pl.pallas_call(
         skipping(pair_sum_body, 3, len(after)),
@@ -314,20 +350,24 @@
 
 
 def ortho_body(place_ref, mine, theirs, out_ref):
-    left = halves_joined(place_ref, mine, theirs) * 0.125
-    gram = lax.dot_general(left, left, NT, precision=highest, preferred_element_type=f32)
+    left = (halves_joined(place_ref, mine, theirs) * 0.125).astype(bf16)
+    gram = dot(left, left, NT)
     row_id = lax.broadcasted_iota(jnp.int32, (R, R), 0)
-    col_id = lax.broadcasted_iota(jnp.int32, (R, R), 1)
-    work = jnp.concatenate([gram, (row_id == col_id).astype(f32)], axis=1)
-    row_ids = lax.broadcasted_iota(jnp.int32, (R, 2 * R), 0)
-    for k in range(R):
-        scale = lax.rsqrt(work[k : k + 1, k : k + 1])
-        row = work[k : k + 1, :] * scale
-        col = work[:, k : k + 1] * scale
-        work = jnp.where(row_ids > k, work - col * row, jnp.where(row_ids == k, row, work))
-    inverse = work[:, R:]
-    out_ref[...] = lax.dot_general(
-        inverse, left, NN, precision=highest, preferred_element_type=f32
+    eye = row_id == lax.broadcasted_iota(jnp.int32, (R, R), 1)
+    work = jnp.concatenate([gram, eye.astype(f32)], axis=1)
+    below = lax.broadcasted_iota(jnp.int32, (R, 1), 0)
+    for k in range(R - 1):
+        col = jnp.where(below > k, work[:, k : k + 1], 0.0)
+        work -= (col * (1.0 / work[k : k + 1, k : k + 1])) * work[k : k + 1, :]
+    pivots = jnp.sum(jnp.where(eye, work[:, :R], 0.0), axis=1, keepdims=True)
+    inverse = work[:, R:] * lax.rsqrt(pivots)
+    parts = []
+    for _ in range(3):
+        parts.append(inverse.astype(bf16))
+        inverse -= parts[-1].astype(f32)
+    product = dot(jnp.concatenate(parts, axis=0), left, NN)
+    out_ref[...] = (
+        product[:R] + (product[R : 2 * R] + product[2 * R :])
     ).astype(bf16)
 
 
@@ -343,61 +383,53 @@
     )(place, mine, theirs, *after)
 
 
-def right_body(left_ref, high_ref, out_ref, total_ref):
-    i = pl.program_id(0)
-    term = dot(left_ref[...], high_ref[...], NN)
-
-    @pl.when(i == 0)
-    def _():
-        total_ref[...] = term
-
-    @pl.when(i > 0)
-    def _():
-        total_ref[...] += term
-
-    @pl.when(i == D // DEEP - 1)
-    def _():
-        out_ref[...] = total_ref[...].astype(bf16)
+def right_body(left_ref, high_ref, out_ref):
+    total = jnp.zeros((R, WIDE), f32)
+    for i in range(D // DEEP):
+        at = slice(i * DEEP, (i + 1) * DEEP)
+        total += dot(left_ref[:, at], high_ref[at], NN)
+    out_ref[...] = total.astype(bf16)
 
 
 def right(left, high, after=()):
     return pl.pallas_call(
         skipping(right_body, 2, len(after)),
-        grid=(D // DEEP,),
-        in_specs=[
-            pl.BlockSpec((R, DEEP), lambda i: (0, i)),
-            pl.BlockSpec((DEEP, WIDE), lambda i: (i, 0)),
-        ]
-        + [ANY] * len(after),
-        out_specs=pl.BlockSpec((R, WIDE), lambda i: (0, 0)),
+        in_specs=[VM, VM] + [ANY] * len(after),
+        out_specs=VM,
         out_shape=jax.ShapeDtypeStruct((R, WIDE), bf16),
-        scratch_shapes=[pltpu.VMEM((R, WIDE), f32)],
         compiler_params=params(8),
         cost_estimate=LITTLE,
         name="right",
     )(left, high, *after)
 
 
-def error_body(left_ref, high_ref, low_ref, mine, theirs, q_ref, out_ref):
+def error_body(left_ref, high_ref, low_ref, mine, theirs, q_ref, error_hbm, error_ref, sems):
     q_next = (mine[...].astype(f32) + theirs[...].astype(f32)) * 0.125
     q_ref[...] = q_next
-    approx = dot(left_ref[...], q_next.astype(bf16), TN)
-    out_ref[0] = (
-        (high_ref[...].astype(f32) - approx) + low_ref[...].astype(f32)
-    ).astype(bf16)
+    q_round = q_next.astype(bf16)
+    copies = []
+    for i in range(D // DEEP):
+        at = pl.ds(i * DEEP, DEEP)
+        approx = dot(left_ref[:, at], q_round, TN)
+        error_ref[at] = (
+            (high_ref[at].astype(f32) - approx) + low_ref[at].astype(f32)
+        ).astype(bf16)
+        copies.append(pltpu.make_async_copy(error_ref.at[at], error_hbm.at[0, at], sems.at[i]))
+        copies[-1].start()
+    for copy in copies:
+        copy.wait()
 
 
 def error(left, high, low, mine, theirs):
-    wide = pl.BlockSpec((DEEP, WIDE), lambda i: (i, 0))
     return pl.pallas_call(
         error_body,
-        grid=(D // DEEP,),
-        in_specs=[pl.BlockSpec((R, DEEP), lambda i: (0, i)), wide, wide, VM, VM],
-        out_specs=[VM, pl.BlockSpec((1, DEEP, WIDE), lambda i: (0, i, 0))],
+        in_specs=[VM] * 5,
+        out_specs=[VM, HBM],
         out_shape=[
             jax.ShapeDtypeStruct((R, WIDE), f32),
             jax.ShapeDtypeStruct((1, D, WIDE), bf16),
         ],
+        scratch_shapes=[pltpu.VMEM((D, WIDE), bf16), pltpu.SemaphoreType.DMA((D // DEEP,))],
         compiler_params=params(14),
         cost_estimate=LITTLE,
         name="error",
@@ -434,23 +466,22 @@
     q_t = q_factors.T
 
     grad, far_x, far_y, weight = gate(
-        place, log_ratios.T, tokens, in_hbm(gate_weight), hidden_grad, up_values
+        place, in_hbm(log_ratios.T), tokens, in_hbm(gate_weight), hidden_grad, up_values
     )
     far_x, far_y = send_on(far_x, "x"), send_on(far_y, "y")
     swapped = swap(grad)
     mine_x, mine_y, own_x, own_y = terms((NEAR, OWN), place, grad, weight)
-    near_x, near_y = terms((NEAR,), place, swapped, weight, (mine_x,))
-    m = near_x
-    near_x, near_y = send_on(near_x, "x"), send_on(near_y, "y")
-    high, low, left_local = merge(tokens, grad, error_feedback, q_t, after=(m,))
+    m, near_y = terms((NEAR,), place, swapped, weight, (mine_x,))
+    near_x, near_y = send_on(m, "x"), send_on(near_y, "y")
+    high, low, left_local = merge(tokens, grad, error_feedback, q_t, (m,))
     message_x = add(mine_x, far_x, (left_local,))
     message_y = add(mine_y, far_y, (message_x,))
     last_x, last_y = send_on(message_x, "x"), send_on(message_y, "y")
     part = pair_sum(place, left_local, (message_y,))
     near_x, near_y, part = lax.optimization_barrier((near_x, near_y, part))
     near_x, near_y = swap(near_x), swap(near_y)
-    part = add(part, from_chip(part, False))
-    part = add(part, from_chip(part, True))
+    part = add(part, from_neighbour(part, False))
+    part = add(part, from_neighbour(part, True))
 
     def across(axis):
         return "y" if axis == "x" else "x"
@@ -460,14 +491,13 @@
     here_y, other_y, this_y, far_y = own("y", place, own_y, last_y, near_y, (here_x,))
     far_y, other_y = send(far_y, across("y"), 2), swap(other_y)
     left = ortho(place, part, swap(part), (here_y,))
-    right_local = right(left, high, (far_x, far_y))
-    part = from_chip(right_local, False)
-    next_x = send_on(pack(this_x, other_x, (right_local,)), across("x"))
-    next_y = send_on(pack(this_y, other_y, (right_local,)), across("y"))
-    part = add(right_local, part)
-    part = add(part, from_chip(part, True))
-    next_x, next_y, part = lax.optimization_barrier((next_x, next_y, part))
-    q_next, error_next = error(left, high, low, part, swap(part))
+    part = right(left, high)
+    next_x = send_on(pack(this_x, other_x, (part, far_x)), across("x"))
+    next_y = send_on(pack(this_y, other_y, (part, far_y)), across("y"))
+    part = chips_sum((part, from_chip(part, 1), from_chip(part, 2), from_chip(part, 3)))
+    theirs = swap(part)
+    next_x, next_y, theirs = lax.optimization_barrier((next_x, next_y, theirs))
+    q_next, error_next = error(left, high, low, part, theirs)
     across_x = (here_x, far_x, next_x, swap(next_x))
     across_y = (here_y, far_y, next_y, swap(next_y))
     token_grad = pl.pallas_call(

time: 115 us -> 107 us (0.930)
  Pallas kernels: 63.6 us -> 58.8 us
  starting transfers between devices: 33 us -> 31.6 us
    ppermute x4 -> x3, waiting for transfers between devices: 10.2 us -> 2.6 us  [from_chip(): return lax.ppermute(array, 'dp', to)]
    ppermute x0 -> x2, waiting for transfers between devices: none -> 6.39 us  [from_neighbour(): return lax.ppermute(array, 'dp', to)]
    ppermute x0 -> x2, starting transfers between devices: none -> 5.11 us  [from_neighbour(): return lax.ppermute(array, 'dp', to)]
    ppermute x4 -> x3, starting transfers between devices: 10.2 us -> 5.73 us  [from_chip(): return lax.ppermute(array, 'dp', to)]
    pallas_call x4 -> x5, Pallas kernels: 44.3 us -> 40.7 us  [the longest x1 18.7 us: gate(): pl.pallas_call(gate_body, in_specs=[SM, HBM, HBM, HBM, HBM, HBM], out_spe...]
    ppermute x8, starting transfers between devices: 13.6 us -> 10.9 us  [send_on(): return lax.ppermute(array, ('dp', 'tensor'), to)]
    ppermute x10, starting transfers between devices: 5.69 us -> 8.41 us  [swap(): return lax.ppermute(array, 'dp', to_core())]
    ppermute x2, starting transfers between devices: 3.52 us -> 1.48 us  [send(): return lax.ppermute(array, 'tensor', to)]
  transfers between devices with their start and end apart: 24 -> 25, of which waited for: 8 -> 9; matrix products, arithmetic and copies ran while one was open for 0% -> 0% of each run, Pallas kernels for 37% -> 35%
where the time goes in v2:
time: 107 us
  Pallas kernels  58.8 us (55%)
  starting transfers between devices  31.6 us (30%)
  waiting for transfers between devices  16 us (15%)
    pallas_call x1, Pallas kernels, gate(): pl.pallas_call(gate_body, in_specs=[SM, HBM, HBM, HBM, HBM, HBM], out_spe...  18.7 us
    pallas_call x1, Pallas kernels, merge(): pl.pallas_call(skipping(merge_body, 4, len(after)), grid=(D // DEEP,), in...  16.5 us
    ppermute x8, starting transfers between devices, send_on(): return lax.ppermute(array, ('dp', 'tensor'), to)  10.9 us
    pallas_call x2, Pallas kernels, terms(): pl.pallas_call(body, in_specs=[SM, VM, VM] + [ANY] * len(after), out_spec...  9.61 us
    ppermute x10, starting transfers between devices, swap(): return lax.ppermute(array, 'dp', to_core())  8.41 us
    ppermute x2, waiting for transfers between devices, from_neighbour(): return lax.ppermute(array, 'dp', to)  6.39 us
    ppermute x3, starting transfers between devices, from_chip(): return lax.ppermute(array, 'dp', to)  5.73 us
    ppermute x2, starting transfers between devices, from_neighbour(): return lax.ppermute(array, 'dp', to)  5.11 us
  transfers between devices with their start and end apart: 25, of which 9 were waited for; matrix products, arithmetic and copies ran while one was open for 0% of the time, Pallas kernels for 35%

profile of v2, /device:TPU:1, one launch (start us, length us, event | category | flops | bytes accessed | tf_op | source)
XLA Modules:
  0.0 107.3 jit_solution(17270724974617665832)
XLA Ops:
  0.6 0.1 pad_add_fusion.place_ref.refs_0_
  0.7 18.7 %gate.1 = (bf16[1280,896]{1,0:T(8,128)(2,1)S(1)}, bf16[4,640,256]{2,1,0:T(8,128)(2,1)S(1)}, bf16[4,640,256]{2,1,0:T(8,128)(2,1)S(1)}, bf16[4096,896]{1,0:T(8,128)(2,1)S(1)}) custom-call(s32[3]{0:T(128)S(1)} %pad_add_fusion.place_ref.refs_0_, f32[2,8]{1,0:T(2,128)} %bitcast.7, bf16[1280,4096]{1,0:T(8,128)(2,1)} %refs_0_.1, bf16[4096,896]{1,0:T(8,128)(2,1)} %weight_hbm.1, ...), custom_call_target="tpu_custom_call" | custom-call | flops 1 | bytes 1 | tf_op jit(solution)/shard_map/gate/pallas_call | solution.py:158
  19.4 1.5 %collective-permute-start.1 = (bf16[1280,896]{1,0:T(8,128)(2,1)S(1)}, bf16[1280,896]{1,0:T(8,128)(2,1)S(1)}, u32[]{:S(2)}, u32[]{:S(2)}) collective-permute-start(bf16[1280,896]{1,0:T(8,128)(2,1)S(1)} %get-tuple-element.32.grad_ref.refs_1_), channel_id=1, source_target_pairs={{0,16},{16,0},{32,48},{48,32},{64,80},{80,64},{96,112},{112,96},{1... | collective-permute-start | bytes 6881288 | tf_op jit(solution)/shard_map/ppermute | solution.py:309
  20.9 2.6 %collective-permute-start = (bf16[4,640,256]{2,1,0:T(8,128)(2,1)S(1)}, bf16[4,640,256]{2,1,0:T(8,128)(2,1)S(1)}, u32[]{:S(2)}, u32[]{:S(2)}) collective-permute-start(bf16[4,640,256]{2,1,0:T(8,128)(2,1)S(1)} %get-tuple-element.36), channel_id=1, source_target_pairs={{0,1},{1,2},{2,3},{3,0},{4,5},{5,6},{6,7},{7,4},{8,9},{9,10},{10,1... | collective-permute-start | bytes 3932168 | tf_op jit(solution)/shard_map/ppermute | solution.py:460
  23.5 2.7 %collective-permute-start.6 = (bf16[4,640,256]{2,1,0:T(8,128)(2,1)S(1)}, bf16[4,640,256]{2,1,0:T(8,128)(2,1)S(1)}, u32[]{:S(2)}, u32[]{:S(2)}) collective-permute-start(bf16[4,640,256]{2,1,0:T(8,128)(2,1)S(1)} %get-tuple-element.41), channel_id=1, source_target_pairs={{0,4},{1,5},{2,6},{3,7},{4,8},{5,9},{6,10},{7,11},{8,12},{9,13},{1... | collective-permute-start | bytes 3932168 | tf_op jit(solution)/shard_map/ppermute | solution.py:460
  26.2 6.2 %terms.2 = (bf16[4,640,256]{2,1,0:T(8,128)(2,1)S(1)}, bf16[4,640,256]{2,1,0:T(8,128)(2,1)S(1)}, bf16[4,640,256]{2,1,0:T(8,128)(2,1)S(1)}, bf16[4,640,256]{2,1,0:T(8,128)(2,1)S(1)}) custom-call(s32[3]{0:T(128)S(1)} %pad_add_fusion.place_ref.refs_0_, bf16[1280,896]{1,0:T(8,128)(2,1)S(1)} %get-tuple-element.32.grad_ref.refs_1_, ...), custom_call_target="tpu_custom_call" | custom-call | flops 1 | bytes 1 | tf_op jit(solution)/shard_map/terms/pallas_call | solution.py:183
  32.4 0.0 collective-permute-done.1.grad_ref
  32.4 0.0 copy-start
  32.4 3.5 %terms.3 = (bf16[4,640,256]{2,1,0:T(8,128)(2,1)S(1)}, bf16[4,640,256]{2,1,0:T(8,128)(2,1)S(1)}) custom-call(s32[3]{0:T(128)S(1)} %pad_add_fusion.place_ref.refs_0_, bf16[1280,896]{1,0:T(8,128)(2,1)S(1)} %collective-permute-done.1.grad_ref, bf16[4096,896]{1,0:T(8,128)(2,1)S(1)} %get-tuple-element.33.weight_ref, bf16[4,640,256]{2,1,0:T(8,128)(2,1)S(1)} %get-tuple-element.35.refs_0_), custom_call_target="tpu_custom_call" | custom-call | flops 1 | bytes 1 | tf_op jit(solution)/shard_map/terms/pallas_call | solution.py:183
  35.8 0.6 collective-permute-start.3
  36.5 0.5 collective-permute-start.4
  36.9 16.5 %merge.1 = (bf16[4096,896]{1,0:T(8,128)(2,1)S(1)}, bf16[4096,896]{1,0:T(8,128)(2,1)S(1)}, bf16[32,4096]{1,0:T(8,128)(2,1)S(1)}) custom-call(bf16[1280,4096]{1,0:T(8,128)(2,1)} %refs_0_.1, bf16[1280,896]{1,0:T(8,128)(2,1)S(1)} %get-tuple-element.32.grad_ref.refs_1_, bf16[1,4096,896]{2,1,0:T(8,128)(2,1)} %refs_2_.1, f32[32,896]{1,0:T(8,128)S(1)} %bitcast.6, ...), custom_call_target="tpu_custom_call" | custom-call | flops 1 | bytes 1 | tf_op jit(solution)/shard_map/merge/pallas_call | solution.py:266
  53.4 0.1 collective-permute-start.5
  53.5 0.0 collective-permute-done.refs_1_
  53.5 0.3 add.8.refs_2_
  53.8 1.5 %collective-permute-start.2 = (bf16[4,640,256]{2,1,0:T(8,128)(2,1)S(1)}, bf16[4,640,256]{2,1,0:T(8,128)(2,1)S(1)}, u32[]{:S(2)}, u32[]{:S(2)}) collective-permute-start(bf16[4,640,256]{2,1,0:T(8,128)(2,1)S(1)} %add.8.refs_2_), channel_id=1, source_target_pairs={{0,1},{1,2},{2,3},{3,0},{4,5},{5,6},{6,7},{7,4},{8,9},{9,10},{10,1... | collective-permute-start | bytes 3932168 | tf_op jit(solution)/shard_map/ppermute | solution.py:460
  55.3 0.0 collective-permute-done.6.refs_1_
  55.3 0.3 add.9.refs_3_
  55.7 0.0 collective-permute-done.5.refs_2_
  55.7 0.6 pair_sum.1.refs_0_
  56.3 0.0 collective-permute-done.3
  56.3 0.0 collective-permute-done.4
  56.3 0.3 collective-permute-start.7
  56.6 1.3 %collective-permute-start.13 = (bf16[4,640,256]{2,1,0:T(8,128)(2,1)S(1)}, bf16[4,640,256]{2,1,0:T(8,128)(2,1)S(1)}, u32[]{:S(2)}, u32[]{:S(2)}) collective-permute-start(bf16[4,640,256]{2,1,0:T(8,128)(2,1)S(1)} %add.9.refs_3_), channel_id=1, source_target_pairs={{0,4},{1,5},{2,6},{3,7},{4,8},{5,9},{6,10},{7,11},{8,12},{9,13},{1... | collective-permute-start | bytes 3932168 | tf_op jit(solution)/shard_map/ppermute | solution.py:460
  57.9 0.3 collective-permute-start.14
  58.2 1.6 %collective-permute-start.8 = (bf16[16,4096]{1,0:T(8,128)(2,1)S(1)}, bf16[16,4096]{1,0:T(8,128)(2,1)S(1)}, u32[]{:S(2)}, u32[]{:S(2)}) collective-permute-start(bf16[16,4096]{1,0:T(8,128)(2,1)S(1)} %pair_sum.1.refs_0_), channel_id=1, source_target_pairs={{0,32},{16,48},{32,0},{48,16},{64,96},{80,112},{96,64},{112,80},{1... | collective-permute-start | bytes 393224 | tf_op jit(solution)/shard_map/ppermute | solution.py:320
  59.8 3.6 %collective-permute-done.8.refs_1_ = bf16[16,4096]{1,0:T(8,128)(2,1)S(1)} collective-permute-done((bf16[16,4096]{1,0:T(8,128)(2,1)S(1)}, bf16[16,4096]{1,0:T(8,128)(2,1)S(1)}, u32[]{:S(2)}, u32[]{:S(2)}) %collective-permute-start.8) | collective-permute-done | bytes 131104 | tf_op jit(solution)/shard_map/ppermute | solution.py:320
  63.5 3.5 %collective-permute-start.9 = (bf16[16,4096]{1,0:T(8,128)(2,1)S(1)}, bf16[16,4096]{1,0:T(8,128)(2,1)S(1)}, u32[]{:S(2)}, u32[]{:S(2)}) collective-permute-start(bf16[16,4096]{1,0:T(8,128)(2,1)S(1)} %add.10.refs_0_), channel_id=1, source_target_pairs={{0,96},{16,112},{32,64},{48,80},{64,32},{80,48},{96,0},{112,16},{1... | collective-permute-start | bytes 393224 | tf_op jit(solution)/shard_map/ppermute | solution.py:320
  66.9 2.8 %collective-permute-done.9.refs_1_ = bf16[16,4096]{1,0:T(8,128)(2,1)S(1)} collective-permute-done((bf16[16,4096]{1,0:T(8,128)(2,1)S(1)}, bf16[16,4096]{1,0:T(8,128)(2,1)S(1)}, u32[]{:S(2)}, u32[]{:S(2)}) %collective-permute-start.9) | collective-permute-done | bytes 131104 | tf_op jit(solution)/shard_map/ppermute | solution.py:320
  69.7 0.9 collective-permute-done.2.refs_2_
  70.6 0.0 collective-permute-done.7.refs_3_
  70.6 1.0 own_x.1
  71.7 1.7 %collective-permute-done.13.refs_2_ = bf16[4,640,256]{2,1,0:T(8,128)(2,1)S(1)} collective-permute-done((bf16[4,640,256]{2,1,0:T(8,128)(2,1)S(1)}, bf16[4,640,256]{2,1,0:T(8,128)(2,1)S(1)}, u32[]{:S(2)}, u32[]{:S(2)}) %collective-permute-start.13) | collective-permute-done | bytes 1310752 | tf_op jit(solution)/shard_map/ppermute | solution.py:460
  73.4 0.0 collective-permute-done.14.refs_3_
  73.4 1.1 own_y.1
  74.5 2.6 %collective-permute-start.16 = (bf16[640,256]{1,0:T(8,128)(2,1)S(1)}, bf16[640,256]{1,0:T(8,128)(2,1)S(1)}, u32[]{:S(2)}, u32[]{:S(2)}) collective-permute-start(bf16[640,256]{1,0:T(8,128)(2,1)S(1)} %get-tuple-element.53), channel_id=1, source_target_pairs={{0,16},{16,0},{32,48},{48,32},{64,80},{80,64},{96,112},{112,96},{1... | collective-permute-start | bytes 983048 | tf_op jit(solution)/shard_map/ppermute | solution.py:309
  77.1 1.3 %collective-permute-start.17 = (bf16[640,256]{1,0:T(8,128)(2,1)S(1)}, bf16[640,256]{1,0:T(8,128)(2,1)S(1)}, u32[]{:S(2)}, u32[]{:S(2)}) collective-permute-start(bf16[640,256]{1,0:T(8,128)(2,1)S(1)} %get-tuple-element.54), channel_id=1, source_target_pairs={{0,2},{1,3},{2,0},{3,1},{4,6},{5,7},{6,4},{7,5},{8,10},{9,11},{10,... | collective-permute-start | bytes 983048 | tf_op jit(solution)/shard_map/ppermute | solution.py:452
  78.4 0.2 collective-permute-start.10
  78.6 0.6 collective-permute-start.11
  79.2 0.0 collective-permute-start.12
  79.2 1.4 %collective-permute-done.12.refs_2_ = bf16[16,4096]{1,0:T(8,128)(2,1)S(1)} collective-permute-done((bf16[16,4096]{1,0:T(8,128)(2,1)S(1)}, bf16[16,4096]{1,0:T(8,128)(2,1)S(1)}, u32[]{:S(2)}, u32[]{:S(2)}) %collective-permute-start.12) | collective-permute-done | bytes 131104 | tf_op jit(solution)/shard_map/ppermute | solution.py:309
  80.6 3.9 %ortho.1.refs_0_.left_ref = bf16[32,4096]{1,0:T(8,128)(2,1)S(1)} custom-call(s32[3]{0:T(128)S(1)} %pad_add_fusion.place_ref.refs_0_, bf16[16,4096]{1,0:T(8,128)(2,1)S(1)} %add.11.refs_4_.refs_1_, bf16[16,4096]{1,0:T(8,128)(2,1)S(1)} %collective-permute-done.12.refs_2_, bf16[640,256]{1,0:T(8,128)(2,1)S(1)} %get-tuple-element.50.refs_3_.refs_4_), custom_call_target="tpu_custom_call" | custom-call | flops 1 | bytes 1 | tf_op jit(solution)/shard_map/ortho/pallas_call | solution.py:375
  84.5 1.3 %right.1.refs_2_.refs_0_ = bf16[32,896]{1,0:T(8,128)(2,1)S(1)} custom-call(bf16[32,4096]{1,0:T(8,128)(2,1)S(1)} %ortho.1.refs_0_.left_ref, bf16[4096,896]{1,0:T(8,128)(2,1)S(1)} %get-tuple-element.51.refs_1_.high_ref), custom_call_target="tpu_custom_call" | custom-call | flops 1 | bytes 1 | tf_op jit(solution)/shard_map/right/pallas_call | solution.py:395
  85.8 0.0 collective-permute-done.16.refs_1_
  85.8 2.0 %collective-permute-done.17.refs_3_.refs_5_ = bf16[640,256]{1,0:T(8,128)(2,1)S(1)} collective-permute-done((bf16[640,256]{1,0:T(8,128)(2,1)S(1)}, bf16[640,256]{1,0:T(8,128)(2,1)S(1)}, u32[]{:S(2)}, u32[]{:S(2)}) %collective-permute-start.17) | collective-permute-done | bytes 327712 | tf_op jit(solution)/shard_map/ppermute | solution.py:452
  87.9 1.7 %collective-permute-start.18 = (bf16[2,640,256]{2,1,0:T(8,128)(2,1)S(1)}, bf16[2,640,256]{2,1,0:T(8,128)(2,1)S(1)}, u32[]{:S(2)}, u32[]{:S(2)}) collective-permute-start(bf16[2,640,256]{2,1,0:T(8,128)(2,1)S(1)} %pack.3), channel_id=1, source_target_pairs={{0,1},{1,2},{2,3},{3,0},{4,5},{5,6},{6,7},{7,4},{8,9},{9,10},{10,1... | collective-permute-start | bytes 1966088 | tf_op jit(solution)/shard_map/ppermute | solution.py:460
  89.6 0.0 collective-permute-done.10.refs_3_.refs_1_
  89.6 0.0 collective-permute-done.11.refs_1_
  89.6 0.1 collective-permute-start.15
  89.7 1.7 %collective-permute-start.19 = (bf16[32,896]{1,0:T(8,128)(2,1)S(1)}, bf16[32,896]{1,0:T(8,128)(2,1)S(1)}, u32[]{:S(2)}, u32[]{:S(2)}) collective-permute-start(bf16[32,896]{1,0:T(8,128)(2,1)S(1)} %right.1.refs_2_.refs_0_), channel_id=1, source_target_pairs={{0,32},{16,48},{32,64},{48,80},{64,96},{80,112},{96,0},{112,16},{1... | collective-permute-start | bytes 172040 | tf_op jit(solution)/shard_map/ppermute | solution.py:314
  91.4 3.3 %collective-permute-start.20 = (bf16[32,896]{1,0:T(8,128)(2,1)S(1)}, bf16[32,896]{1,0:T(8,128)(2,1)S(1)}, u32[]{:S(2)}, u32[]{:S(2)}) collective-permute-start(bf16[32,896]{1,0:T(8,128)(2,1)S(1)} %right.1.refs_2_.refs_0_), channel_id=1, source_target_pairs={{0,64},{16,80},{32,96},{48,112},{64,0},{80,16},{96,32},{112,48},{1... | collective-permute-start | bytes 172040 | tf_op jit(solution)/shard_map/ppermute | solution.py:314
  94.7 0.7 collective-permute-start.21
  95.4 0.0 collective-permute-done.19.refs_1_
  95.4 1.8 %collective-permute-done.20.refs_2_ = bf16[32,896]{1,0:T(8,128)(2,1)S(1)} collective-permute-done((bf16[32,896]{1,0:T(8,128)(2,1)S(1)}, bf16[32,896]{1,0:T(8,128)(2,1)S(1)}, u32[]{:S(2)}, u32[]{:S(2)}) %collective-permute-start.20) | collective-permute-done | bytes 57376 | tf_op jit(solution)/shard_map/ppermute | solution.py:314
  97.2 0.8 collective-permute-done.21.refs_3_
  98.1 1.9 %collective-permute-start.22 = (bf16[32,896]{1,0:T(8,128)(2,1)S(1)}, bf16[32,896]{1,0:T(8,128)(2,1)S(1)}, u32[]{:S(2)}, u32[]{:S(2)}) collective-permute-start(bf16[32,896]{1,0:T(8,128)(2,1)S(1)} %chips_sum.1.mine), channel_id=1, source_target_pairs={{0,16},{16,0},{32,48},{48,32},{64,80},{80,64},{96,112},{112,96},{1... | collective-permute-start | bytes 172040 | tf_op jit(solution)/shard_map/ppermute | solution.py:309
  100.0 0.9 collective-permute-done.22.theirs
  100.9 0.0 collective-permute-done.18.refs_6_
  100.9 0.0 collective-permute-done.15.refs_2_
  100.9 1.0 collective-permute-start.23
  101.9 0.0 collective-permute-start.24
  101.9 4.2 %error.1 = (f32[32,896]{1,0:T(8,128)}, bf16[1,4096,896]{2,1,0:T(8,128)(2,1)}) custom-call(bf16[32,4096]{1,0:T(8,128)(2,1)S(1)} %ortho.1.refs_0_.left_ref, bf16[4096,896]{1,0:T(8,128)(2,1)S(1)} %get-tuple-element.51.refs_1_.high_ref, bf16[4096,896]{1,0:T(8,128)(2,1)S(1)} %get-tuple-element.57.low_ref, bf16[32,896]{1,0:T(8,128)(2,1)S(1)} %chips_sum.1.mine, ...), custom_call_target="tpu_custom_call" | custom-call | flops 1 | bytes 1 | tf_op jit(solution)/shard_map/error/pallas_call | solution.py:424
  106.2 0.0 collective-permute-done.24.refs_7_
  106.2 1.2 %add_terms.1 = bf16[1280,256]{1,0:T(8,128)(2,1)} custom-call(bf16[640,256]{1,0:T(8,128)(2,1)S(1)} %get-tuple-element.44.refs_4_.refs_0_, bf16[640,256]{1,0:T(8,128)(2,1)S(1)} %collective-permute-done.10.refs_3_.refs_1_, bf16[2,640,256]{2,1,0:T(8,128)(2,1)S(1)} %collective-permute-done.15.refs_2_, bf16[2,640,256]{2,1,0:T(8,128)(2,1)S(1)} %collective-permute-done.23.refs_3_, ...), custom_call_target="tpu_custom_call" | custom-call | flops 1 | bytes 1 | tf_op jit(solution)/shard_map/add_terms/pallas_call | solution.py:503
  (7 shorter events, 0.2 us)
Async XLA Ops:
  19.4 13.0 %collective-permute-start.1 = (bf16[1280,896]{1,0:T(8,128)(2,1)S(1)}, bf16[1280,896]{1,0:T(8,128)(2,1)S(1)}, u32[]{:S(2)}, u32[]{:S(2)}) collective-permute-start(bf16[1280,896]{1,0:T(8,128)(2,1)S(1)} %get-tuple-element.32.grad_ref.refs_1_), channel_id=1, source_target_pairs={{0,16},{16,0},{32,48},{48,32},{64,80},{80,64},{96,112},{112,96},{1... | collective-permute-start | bytes 6881288 | tf_op jit(solution)/shard_map/ppermute | solution.py:309
  20.9 32.6 %collective-permute-start = (bf16[4,640,256]{2,1,0:T(8,128)(2,1)S(1)}, bf16[4,640,256]{2,1,0:T(8,128)(2,1)S(1)}, u32[]{:S(2)}, u32[]{:S(2)}) collective-permute-start(bf16[4,640,256]{2,1,0:T(8,128)(2,1)S(1)} %get-tuple-element.36), channel_id=1, source_target_pairs={{0,1},{1,2},{2,3},{3,0},{4,5},{5,6},{6,7},{7,4},{8,9},{9,10},{10,1... | collective-permute-start | bytes 3932168 | tf_op jit(solution)/shard_map/ppermute | solution.py:460
  23.5 31.8 %collective-permute-start.6 = (bf16[4,640,256]{2,1,0:T(8,128)(2,1)S(1)}, bf16[4,640,256]{2,1,0:T(8,128)(2,1)S(1)}, u32[]{:S(2)}, u32[]{:S(2)}) collective-permute-start(bf16[4,640,256]{2,1,0:T(8,128)(2,1)S(1)} %get-tuple-element.41), channel_id=1, source_target_pairs={{0,4},{1,5},{2,6},{3,7},{4,8},{5,9},{6,10},{7,11},{8,12},{9,13},{1... | collective-permute-start | bytes 3932168 | tf_op jit(solution)/shard_map/ppermute | solution.py:460
  32.4 4.6 %copy-start = (f32[896,32]{0,1:T(8,128)S(1)}, f32[896,32]{0,1:T(8,128)}, u32[]{:S(2)}) copy-start(f32[896,32]{0,1:T(8,128)} %param.12) | copy-start | bytes 344068
  35.8 20.4 %collective-permute-start.3 = (bf16[4,640,256]{2,1,0:T(8,128)(2,1)S(1)}, bf16[4,640,256]{2,1,0:T(8,128)(2,1)S(1)}, u32[]{:S(2)}, u32[]{:S(2)}) collective-permute-start(bf16[4,640,256]{2,1,0:T(8,128)(2,1)S(1)} %get-tuple-element.37.refs_4_), channel_id=1, source_target_pairs={{0,1},{1,2},{2,3},{3,0},{4,5},{5,6},{6,7},{7,4},{8,9},{9,10},{10,1... | collective-permute-start | bytes 3932168 | tf_op jit(solution)/shard_map/ppermute | solution.py:460
  36.5 19.8 %collective-permute-start.4 = (bf16[4,640,256]{2,1,0:T(8,128)(2,1)S(1)}, bf16[4,640,256]{2,1,0:T(8,128)(2,1)S(1)}, u32[]{:S(2)}, u32[]{:S(2)}) collective-permute-start(bf16[4,640,256]{2,1,0:T(8,128)(2,1)S(1)} %get-tuple-element.39), channel_id=1, source_target_pairs={{0,4},{1,5},{2,6},{3,7},{4,8},{5,9},{6,10},{7,11},{8,12},{9,13},{1... | collective-permute-start | bytes 3932168 | tf_op jit(solution)/shard_map/ppermute | solution.py:460
  53.4 2.2 %collective-permute-start.5 = (bf16[32,4096]{1,0:T(8,128)(2,1)S(1)}, bf16[32,4096]{1,0:T(8,128)(2,1)S(1)}, u32[]{:S(2)}, u32[]{:S(2)}) collective-permute-start(bf16[32,4096]{1,0:T(8,128)(2,1)S(1)} %get-tuple-element.38.refs_2_.refs_1_), channel_id=1, source_target_pairs={{0,16},{16,0},{32,48},{48,32},{64,80},{80,64},{96,112},{112,96},{1... | collective-permute-start | bytes 786440 | tf_op jit(solution)/shard_map/ppermute | solution.py:309
  53.8 16.8 %collective-permute-start.2 = (bf16[4,640,256]{2,1,0:T(8,128)(2,1)S(1)}, bf16[4,640,256]{2,1,0:T(8,128)(2,1)S(1)}, u32[]{:S(2)}, u32[]{:S(2)}) collective-permute-start(bf16[4,640,256]{2,1,0:T(8,128)(2,1)S(1)} %add.8.refs_2_), channel_id=1, source_target_pairs={{0,1},{1,2},{2,3},{3,0},{4,5},{5,6},{6,7},{7,4},{8,9},{9,10},{10,1... | collective-permute-start | bytes 3932168 | tf_op jit(solution)/shard_map/ppermute | solution.py:460
  56.3 14.3 %collective-permute-start.7 = (bf16[4,640,256]{2,1,0:T(8,128)(2,1)S(1)}, bf16[4,640,256]{2,1,0:T(8,128)(2,1)S(1)}, u32[]{:S(2)}, u32[]{:S(2)}) collective-permute-start(bf16[4,640,256]{2,1,0:T(8,128)(2,1)S(1)} %collective-permute-done.3), channel_id=1, source_target_pairs={{0,16},{16,0},{32,48},{48,32},{64,80},{80,64},{96,112},{112,96},{1... | collective-permute-start | bytes 3932168 | tf_op jit(solution)/shard_map/ppermute | solution.py:309
  56.6 16.8 %collective-permute-start.13 = (bf16[4,640,256]{2,1,0:T(8,128)(2,1)S(1)}, bf16[4,640,256]{2,1,0:T(8,128)(2,1)S(1)}, u32[]{:S(2)}, u32[]{:S(2)}) collective-permute-start(bf16[4,640,256]{2,1,0:T(8,128)(2,1)S(1)} %add.9.refs_3_), channel_id=1, source_target_pairs={{0,4},{1,5},{2,6},{3,7},{4,8},{5,9},{6,10},{7,11},{8,12},{9,13},{1... | collective-permute-start | bytes 3932168 | tf_op jit(solution)/shard_map/ppermute | solution.py:460
  57.9 15.5 %collective-permute-start.14 = (bf16[4,640,256]{2,1,0:T(8,128)(2,1)S(1)}, bf16[4,640,256]{2,1,0:T(8,128)(2,1)S(1)}, u32[]{:S(2)}, u32[]{:S(2)}) collective-permute-start(bf16[4,640,256]{2,1,0:T(8,128)(2,1)S(1)} %collective-permute-done.4), channel_id=1, source_target_pairs={{0,16},{16,0},{32,48},{48,32},{64,80},{80,64},{96,112},{112,96},{1... | collective-permute-start | bytes 3932168 | tf_op jit(solution)/shard_map/ppermute | solution.py:309
  58.2 5.2 %collective-permute-start.8 = (bf16[16,4096]{1,0:T(8,128)(2,1)S(1)}, bf16[16,4096]{1,0:T(8,128)(2,1)S(1)}, u32[]{:S(2)}, u32[]{:S(2)}) collective-permute-start(bf16[16,4096]{1,0:T(8,128)(2,1)S(1)} %pair_sum.1.refs_0_), channel_id=1, source_target_pairs={{0,32},{16,48},{32,0},{48,16},{64,96},{80,112},{96,64},{112,80},{1... | collective-permute-start | bytes 393224 | tf_op jit(solution)/shard_map/ppermute | solution.py:320
  63.5 6.3 %collective-permute-start.9 = (bf16[16,4096]{1,0:T(8,128)(2,1)S(1)}, bf16[16,4096]{1,0:T(8,128)(2,1)S(1)}, u32[]{:S(2)}, u32[]{:S(2)}) collective-permute-start(bf16[16,4096]{1,0:T(8,128)(2,1)S(1)} %add.10.refs_0_), channel_id=1, source_target_pairs={{0,96},{16,112},{32,64},{48,80},{64,32},{80,48},{96,0},{112,16},{1... | collective-permute-start | bytes 393224 | tf_op jit(solution)/shard_map/ppermute | solution.py:320
  74.5 11.4 %collective-permute-start.16 = (bf16[640,256]{1,0:T(8,128)(2,1)S(1)}, bf16[640,256]{1,0:T(8,128)(2,1)S(1)}, u32[]{:S(2)}, u32[]{:S(2)}) collective-permute-start(bf16[640,256]{1,0:T(8,128)(2,1)S(1)} %get-tuple-element.53), channel_id=1, source_target_pairs={{0,16},{16,0},{32,48},{48,32},{64,80},{80,64},{96,112},{112,96},{1... | collective-permute-start | bytes 983048 | tf_op jit(solution)/shard_map/ppermute | solution.py:309
  77.1 10.8 %collective-permute-start.17 = (bf16[640,256]{1,0:T(8,128)(2,1)S(1)}, bf16[640,256]{1,0:T(8,128)(2,1)S(1)}, u32[]{:S(2)}, u32[]{:S(2)}) collective-permute-start(bf16[640,256]{1,0:T(8,128)(2,1)S(1)} %get-tuple-element.54), channel_id=1, source_target_pairs={{0,2},{1,3},{2,0},{3,1},{4,6},{5,7},{6,4},{7,5},{8,10},{9,11},{10,... | collective-permute-start | bytes 983048 | tf_op jit(solution)/shard_map/ppermute | solution.py:452
  78.4 11.2 %collective-permute-start.10 = (bf16[640,256]{1,0:T(8,128)(2,1)S(1)}, bf16[640,256]{1,0:T(8,128)(2,1)S(1)}, u32[]{:S(2)}, u32[]{:S(2)}) collective-permute-start(bf16[640,256]{1,0:T(8,128)(2,1)S(1)} %get-tuple-element.45), channel_id=1, source_target_pairs={{0,8},{1,9},{2,10},{3,11},{4,12},{5,13},{6,14},{7,15},{8,0},{9,1},... | collective-permute-start | bytes 983048 | tf_op jit(solution)/shard_map/ppermute | solution.py:452
  78.6 11.0 %collective-permute-start.11 = (bf16[640,256]{1,0:T(8,128)(2,1)S(1)}, bf16[640,256]{1,0:T(8,128)(2,1)S(1)}, u32[]{:S(2)}, u32[]{:S(2)}) collective-permute-start(bf16[640,256]{1,0:T(8,128)(2,1)S(1)} %get-tuple-element.47), channel_id=1, source_target_pairs={{0,16},{16,0},{32,48},{48,32},{64,80},{80,64},{96,112},{112,96},{1... | collective-permute-start | bytes 983048 | tf_op jit(solution)/shard_map/ppermute | solution.py:309
  79.2 1.4 %collective-permute-start.12 = (bf16[16,4096]{1,0:T(8,128)(2,1)S(1)}, bf16[16,4096]{1,0:T(8,128)(2,1)S(1)}, u32[]{:S(2)}, u32[]{:S(2)}) collective-permute-start(bf16[16,4096]{1,0:T(8,128)(2,1)S(1)} %add.11.refs_4_.refs_1_), channel_id=1, source_target_pairs={{0,16},{16,0},{32,48},{48,32},{64,80},{80,64},{96,112},{112,96},{1... | collective-permute-start | bytes 393224 | tf_op jit(solution)/shard_map/ppermute | solution.py:309
  87.9 13.0 %collective-permute-start.18 = (bf16[2,640,256]{2,1,0:T(8,128)(2,1)S(1)}, bf16[2,640,256]{2,1,0:T(8,128)(2,1)S(1)}, u32[]{:S(2)}, u32[]{:S(2)}) collective-permute-start(bf16[2,640,256]{2,1,0:T(8,128)(2,1)S(1)} %pack.3), channel_id=1, source_target_pairs={{0,1},{1,2},{2,3},{3,0},{4,5},{5,6},{6,7},{7,4},{8,9},{9,10},{10,1... | collective-permute-start | bytes 1966088 | tf_op jit(solution)/shard_map/ppermute | solution.py:460
  89.6 11.3 %collective-permute-start.15 = (bf16[2,640,256]{2,1,0:T(8,128)(2,1)S(1)}, bf16[2,640,256]{2,1,0:T(8,128)(2,1)S(1)}, u32[]{:S(2)}, u32[]{:S(2)}) collective-permute-start(bf16[2,640,256]{2,1,0:T(8,128)(2,1)S(1)} %pack.2), channel_id=1, source_target_pairs={{0,4},{1,5},{2,6},{3,7},{4,8},{5,9},{6,10},{7,11},{8,12},{9,13},{1... | collective-permute-start | bytes 1966088 | tf_op jit(solution)/shard_map/ppermute | solution.py:460
  89.7 5.7 %collective-permute-start.19 = (bf16[32,896]{1,0:T(8,128)(2,1)S(1)}, bf16[32,896]{1,0:T(8,128)(2,1)S(1)}, u32[]{:S(2)}, u32[]{:S(2)}) collective-permute-start(bf16[32,896]{1,0:T(8,128)(2,1)S(1)} %right.1.refs_2_.refs_0_), channel_id=1, source_target_pairs={{0,32},{16,48},{32,64},{48,80},{64,96},{80,112},{96,0},{112,16},{1... | collective-permute-start | bytes 172040 | tf_op jit(solution)/shard_map/ppermute | solution.py:314
  91.4 5.8 %collective-permute-start.20 = (bf16[32,896]{1,0:T(8,128)(2,1)S(1)}, bf16[32,896]{1,0:T(8,128)(2,1)S(1)}, u32[]{:S(2)}, u32[]{:S(2)}) collective-permute-start(bf16[32,896]{1,0:T(8,128)(2,1)S(1)} %right.1.refs_2_.refs_0_), channel_id=1, source_target_pairs={{0,64},{16,80},{32,96},{48,112},{64,0},{80,16},{96,32},{112,48},{1... | collective-permute-start | bytes 172040 | tf_op jit(solution)/shard_map/ppermute | solution.py:314
  94.7 3.3 %collective-permute-start.21 = (bf16[32,896]{1,0:T(8,128)(2,1)S(1)}, bf16[32,896]{1,0:T(8,128)(2,1)S(1)}, u32[]{:S(2)}, u32[]{:S(2)}) collective-permute-start(bf16[32,896]{1,0:T(8,128)(2,1)S(1)} %right.1.refs_2_.refs_0_), channel_id=1, source_target_pairs={{0,96},{16,112},{32,0},{48,16},{64,32},{80,48},{96,64},{112,80},{1... | collective-permute-start | bytes 172040 | tf_op jit(solution)/shard_map/ppermute | solution.py:314
  98.1 2.8 %collective-permute-start.22 = (bf16[32,896]{1,0:T(8,128)(2,1)S(1)}, bf16[32,896]{1,0:T(8,128)(2,1)S(1)}, u32[]{:S(2)}, u32[]{:S(2)}) collective-permute-start(bf16[32,896]{1,0:T(8,128)(2,1)S(1)} %chips_sum.1.mine), channel_id=1, source_target_pairs={{0,16},{16,0},{32,48},{48,32},{64,80},{80,64},{96,112},{112,96},{1... | collective-permute-start | bytes 172040 | tf_op jit(solution)/shard_map/ppermute | solution.py:309
  100.9 5.2 %collective-permute-start.23 = (bf16[2,640,256]{2,1,0:T(8,128)(2,1)S(1)}, bf16[2,640,256]{2,1,0:T(8,128)(2,1)S(1)}, u32[]{:S(2)}, u32[]{:S(2)}) collective-permute-start(bf16[2,640,256]{2,1,0:T(8,128)(2,1)S(1)} %collective-permute-done.15.refs_2_), channel_id=1, source_target_pairs={{0,16},{16,0},{32,48},{48,32},{64,80},{80,64},{96,112},{112,96},{1... | collective-permute-start | bytes 1966088 | tf_op jit(solution)/shard_map/ppermute | solution.py:309
  101.9 4.2 %collective-permute-start.24 = (bf16[2,640,256]{2,1,0:T(8,128)(2,1)S(1)}, bf16[2,640,256]{2,1,0:T(8,128)(2,1)S(1)}, u32[]{:S(2)}, u32[]{:S(2)}) collective-permute-start(bf16[2,640,256]{2,1,0:T(8,128)(2,1)S(1)} %collective-permute-done.18.refs_6_), channel_id=1, source_target_pairs={{0,16},{16,0},{32,48},{48,32},{64,80},{80,64},{96,112},{112,96},{1... | collective-permute-start | bytes 1966088 | tf_op jit(solution)/shard_map/ppermute | solution.py:309

commit v3 on v2

--- a/solution.py
+++ b/solution.py
@@ -309,32 +309,10 @@
     return lax.ppermute(array, "dp", to_core())
 
 
-def from_chip(array, d):
-    to = [(2 * z + c, 2 * ((z + d) % SIDE) + c) for z in range(SIDE) for c in range(2)]
-    return lax.ppermute(array, "dp", to)
-
-
 def from_neighbour(array, second):
     ws = (3, 2, 1, 0) if second else (1, 0, 3, 2)
     to = [(2 * z + c, 2 * w + c) for z, w in enumerate(ws) for c in range(2)]
     return lax.ppermute(array, "dp", to)
-
-
-def chips_sum_body(a_ref, b_ref, c_ref, d_ref, out_ref):
-    a, b, c, d = (r[...].astype(f32) for r in (a_ref, b_ref, c_ref, d_ref))
-    out_ref[...] = ((a + c) + (b + d)).astype(bf16)
-
-
-def chips_sum(arrays, after=()):
-    return pl.pallas_call(
-        skipping(chips_sum_body, SIDE, len(after)),
-        in_specs=[VM] * SIDE + [ANY] * len(after),
-        out_specs=VM,
-        out_shape=jax.ShapeDtypeStruct(arrays[0].shape, bf16),
-        compiler_params=params(4),
-        cost_estimate=LITTLE,
-        name="chips_sum",
-    )(*arrays, *after)
 
 
 def pair_sum(place, local, after=()):
@@ -483,18 +461,21 @@
     part = add(part, from_neighbour(part, False))
     part = add(part, from_neighbour(part, True))
 
+    theirs = swap(part)
+
     def across(axis):
         return "y" if axis == "x" else "x"
 
-    here_x, other_x, this_x, far_x = own("x", place, own_x, last_x, near_x, (part,))
+    here_x, other_x, this_x, far_x = own("x", place, own_x, last_x, near_x, (theirs,))
     far_x, other_x = send(far_x, across("x"), 2), swap(other_x)
     here_y, other_y, this_y, far_y = own("y", place, own_y, last_y, near_y, (here_x,))
     far_y, other_y = send(far_y, across("y"), 2), swap(other_y)
-    left = ortho(place, part, swap(part), (here_y,))
+    left = ortho(place, part, theirs, (here_y,))
     part = right(left, high)
-    next_x = send_on(pack(this_x, other_x, (part, far_x)), across("x"))
-    next_y = send_on(pack(this_y, other_y, (part, far_y)), across("y"))
-    part = chips_sum((part, from_chip(part, 1), from_chip(part, 2), from_chip(part, 3)))
+    next_x = send_on(pack(this_x, other_x, (part,)), across("x"))
+    next_y = send_on(pack(this_y, other_y, (part,)), across("y"))
+    part = add(part, from_neighbour(part, False))
+    part = add(part, from_neighbour(part, True))
     theirs = swap(part)
     next_x, next_y, theirs = lax.optimization_barrier((next_x, next_y, theirs))
     q_next, error_next = error(left, high, low, part, theirs)

time: 107 us -> 109 us (1.019)
  waiting for transfers between devices: 16 us -> 17.4 us
    ppermute x3 -> x0, starting transfers between devices: 5.73 us -> none  [from_chip(): return lax.ppermute(array, 'dp', to)]
    ppermute x2 -> x4, starting transfers between devices: 5.11 us -> 10.3 us  [from_neighbour(): return lax.ppermute(array, 'dp', to)]
    ppermute x2 -> x4, waiting for transfers between devices: 6.39 us -> 10.7 us  [from_neighbour(): return lax.ppermute(array, 'dp', to)]
    ppermute x2, waiting for transfers between devices: 2.01 us -> 4.78 us  [send(): return lax.ppermute(array, 'tensor', to)]
    ppermute x8, waiting for transfers between devices: 2.63 us -> 0.02 us  [send_on(): return lax.ppermute(array, ('dp', 'tensor'), to)]
    ppermute x3 -> x0, waiting for transfers between devices: 2.6 us -> none  [from_chip(): return lax.ppermute(array, 'dp', to)]
    ppermute x2, starting transfers between devices: 1.48 us -> 2.95 us  [send(): return lax.ppermute(array, 'tensor', to)]
  transfers between devices with their start and end apart: 25 -> 24, of which waited for: 9 -> 8; matrix products, arithmetic and copies ran while one was open for 0% -> 0% of each run, Pallas kernels for 35% -> 35%
where the time goes in v3:
time: 109 us
  Pallas kernels  58.8 us (54%)
  starting transfers between devices  32.1 us (29%)
  waiting for transfers between devices  17.4 us (16%)
    pallas_call x1, Pallas kernels, gate(): pl.pallas_call(gate_body, in_specs=[SM, HBM, HBM, HBM, HBM, HBM], out_spe...  18.7 us
    pallas_call x1, Pallas kernels, merge(): pl.pallas_call(skipping(merge_body, 4, len(after)), grid=(D // DEEP,), in...  16.5 us
    ppermute x8, starting transfers between devices, send_on(): return lax.ppermute(array, ('dp', 'tensor'), to)  11.2 us
    ppermute x4, waiting for transfers between devices, from_neighbour(): return lax.ppermute(array, 'dp', to)  10.7 us
    ppermute x4, starting transfers between devices, from_neighbour(): return lax.ppermute(array, 'dp', to)  10.3 us
    pallas_call x2, Pallas kernels, terms(): pl.pallas_call(body, in_specs=[SM, VM, VM] + [ANY] * len(after), out_spec...  9.61 us
    ppermute x10, starting transfers between devices, swap(): return lax.ppermute(array, 'dp', to_core())  7.61 us
    ppermute x2, waiting for transfers between devices, send(): return lax.ppermute(array, 'tensor', to)  4.78 us
  transfers between devices with their start and end apart: 24, of which 8 were waited for; matrix products, arithmetic and copies ran while one was open for 0% of the time, Pallas kernels for 35%

profile of v3, /device:TPU:1, one launch (start us, length us, event | category | flops | bytes accessed | tf_op | source)
XLA Modules:
  0.0 109.2 jit_solution(11112528644501782913)
XLA Ops:
  0.6 0.1 pad_add_fusion.place_ref.refs_0_
  0.7 18.7 %gate.1 = (bf16[1280,896]{1,0:T(8,128)(2,1)S(1)}, bf16[4,640,256]{2,1,0:T(8,128)(2,1)S(1)}, bf16[4,640,256]{2,1,0:T(8,128)(2,1)S(1)}, bf16[4096,896]{1,0:T(8,128)(2,1)S(1)}) custom-call(s32[3]{0:T(128)S(1)} %pad_add_fusion.place_ref.refs_0_, f32[2,8]{1,0:T(2,128)} %bitcast.7, bf16[1280,4096]{1,0:T(8,128)(2,1)} %refs_0_.1, bf16[4096,896]{1,0:T(8,128)(2,1)} %weight_hbm.1, ...), custom_call_target="tpu_custom_call" | custom-call | flops 1 | bytes 1 | tf_op jit(solution)/shard_map/gate/pallas_call | solution.py:158
  19.4 1.5 %collective-permute-start.1 = (bf16[1280,896]{1,0:T(8,128)(2,1)S(1)}, bf16[1280,896]{1,0:T(8,128)(2,1)S(1)}, u32[]{:S(2)}, u32[]{:S(2)}) collective-permute-start(bf16[1280,896]{1,0:T(8,128)(2,1)S(1)} %get-tuple-element.32.grad_ref.refs_1_), channel_id=1, source_target_pairs={{0,16},{16,0},{32,48},{48,32},{64,80},{80,64},{96,112},{112,96},{1... | collective-permute-start | bytes 6881288 | tf_op jit(solution)/shard_map/ppermute | solution.py:309
  20.9 2.6 %collective-permute-start = (bf16[4,640,256]{2,1,0:T(8,128)(2,1)S(1)}, bf16[4,640,256]{2,1,0:T(8,128)(2,1)S(1)}, u32[]{:S(2)}, u32[]{:S(2)}) collective-permute-start(bf16[4,640,256]{2,1,0:T(8,128)(2,1)S(1)} %get-tuple-element.36), channel_id=1, source_target_pairs={{0,1},{1,2},{2,3},{3,0},{4,5},{5,6},{6,7},{7,4},{8,9},{9,10},{10,1... | collective-permute-start | bytes 3932168 | tf_op jit(solution)/shard_map/ppermute | solution.py:438
  23.5 2.7 %collective-permute-start.6 = (bf16[4,640,256]{2,1,0:T(8,128)(2,1)S(1)}, bf16[4,640,256]{2,1,0:T(8,128)(2,1)S(1)}, u32[]{:S(2)}, u32[]{:S(2)}) collective-permute-start(bf16[4,640,256]{2,1,0:T(8,128)(2,1)S(1)} %get-tuple-element.41), channel_id=1, source_target_pairs={{0,4},{1,5},{2,6},{3,7},{4,8},{5,9},{6,10},{7,11},{8,12},{9,13},{1... | collective-permute-start | bytes 3932168 | tf_op jit(solution)/shard_map/ppermute | solution.py:438
  26.2 6.2 %terms.2 = (bf16[4,640,256]{2,1,0:T(8,128)(2,1)S(1)}, bf16[4,640,256]{2,1,0:T(8,128)(2,1)S(1)}, bf16[4,640,256]{2,1,0:T(8,128)(2,1)S(1)}, bf16[4,640,256]{2,1,0:T(8,128)(2,1)S(1)}) custom-call(s32[3]{0:T(128)S(1)} %pad_add_fusion.place_ref.refs_0_, bf16[1280,896]{1,0:T(8,128)(2,1)S(1)} %get-tuple-element.32.grad_ref.refs_1_, ...), custom_call_target="tpu_custom_call" | custom-call | flops 1 | bytes 1 | tf_op jit(solution)/shard_map/terms/pallas_call | solution.py:183
  32.4 0.0 collective-permute-done.1.grad_ref
  32.4 0.0 copy-start
  32.4 3.5 %terms.3 = (bf16[4,640,256]{2,1,0:T(8,128)(2,1)S(1)}, bf16[4,640,256]{2,1,0:T(8,128)(2,1)S(1)}) custom-call(s32[3]{0:T(128)S(1)} %pad_add_fusion.place_ref.refs_0_, bf16[1280,896]{1,0:T(8,128)(2,1)S(1)} %collective-permute-done.1.grad_ref, bf16[4096,896]{1,0:T(8,128)(2,1)S(1)} %get-tuple-element.33.weight_ref, bf16[4,640,256]{2,1,0:T(8,128)(2,1)S(1)} %get-tuple-element.35.refs_0_), custom_call_target="tpu_custom_call" | custom-call | flops 1 | bytes 1 | tf_op jit(solution)/shard_map/terms/pallas_call | solution.py:183
  35.8 0.6 collective-permute-start.3
  36.5 0.5 collective-permute-start.4
  36.9 0.0 copy-done
  36.9 16.5 %merge.1 = (bf16[4096,896]{1,0:T(8,128)(2,1)S(1)}, bf16[4096,896]{1,0:T(8,128)(2,1)S(1)}, bf16[32,4096]{1,0:T(8,128)(2,1)S(1)}) custom-call(bf16[1280,4096]{1,0:T(8,128)(2,1)} %refs_0_.1, bf16[1280,896]{1,0:T(8,128)(2,1)S(1)} %get-tuple-element.32.grad_ref.refs_1_, bf16[1,4096,896]{2,1,0:T(8,128)(2,1)} %refs_2_.1, f32[32,896]{1,0:T(8,128)S(1)} %bitcast.6, ...), custom_call_target="tpu_custom_call" | custom-call | flops 1 | bytes 1 | tf_op jit(solution)/shard_map/merge/pallas_call | solution.py:266
  53.4 0.1 collective-permute-start.5
  53.5 0.0 collective-permute-done.refs_1_
  53.5 0.3 add.10.refs_2_
  53.8 1.5 %collective-permute-start.2 = (bf16[4,640,256]{2,1,0:T(8,128)(2,1)S(1)}, bf16[4,640,256]{2,1,0:T(8,128)(2,1)S(1)}, u32[]{:S(2)}, u32[]{:S(2)}) collective-permute-start(bf16[4,640,256]{2,1,0:T(8,128)(2,1)S(1)} %add.10.refs_2_), channel_id=1, source_target_pairs={{0,1},{1,2},{2,3},{3,0},{4,5},{5,6},{6,7},{7,4},{8,9},{9,10},{10,1... | collective-permute-start | bytes 3932168 | tf_op jit(solution)/shard_map/ppermute | solution.py:438
  55.3 0.0 collective-permute-done.6.refs_1_
  55.3 0.3 add.11.refs_3_
  55.7 0.0 collective-permute-done.5.refs_2_
  55.7 0.6 pair_sum.1.refs_0_
  56.3 0.0 collective-permute-done.3
  56.3 0.0 collective-permute-done.4
  56.3 0.3 collective-permute-start.7
  56.6 1.3 %collective-permute-start.13 = (bf16[4,640,256]{2,1,0:T(8,128)(2,1)S(1)}, bf16[4,640,256]{2,1,0:T(8,128)(2,1)S(1)}, u32[]{:S(2)}, u32[]{:S(2)}) collective-permute-start(bf16[4,640,256]{2,1,0:T(8,128)(2,1)S(1)} %add.11.refs_3_), channel_id=1, source_target_pairs={{0,4},{1,5},{2,6},{3,7},{4,8},{5,9},{6,10},{7,11},{8,12},{9,13},{1... | collective-permute-start | bytes 3932168 | tf_op jit(solution)/shard_map/ppermute | solution.py:438
  57.9 0.3 collective-permute-start.14
  58.2 1.6 %collective-permute-start.8 = (bf16[16,4096]{1,0:T(8,128)(2,1)S(1)}, bf16[16,4096]{1,0:T(8,128)(2,1)S(1)}, u32[]{:S(2)}, u32[]{:S(2)}) collective-permute-start(bf16[16,4096]{1,0:T(8,128)(2,1)S(1)} %pair_sum.1.refs_0_), channel_id=1, source_target_pairs={{0,32},{16,48},{32,0},{48,16},{64,96},{80,112},{96,64},{112,80},{1... | collective-permute-start | bytes 393224 | tf_op jit(solution)/shard_map/ppermute | solution.py:315
  59.8 3.6 %collective-permute-done.8.refs_1_ = bf16[16,4096]{1,0:T(8,128)(2,1)S(1)} collective-permute-done((bf16[16,4096]{1,0:T(8,128)(2,1)S(1)}, bf16[16,4096]{1,0:T(8,128)(2,1)S(1)}, u32[]{:S(2)}, u32[]{:S(2)}) %collective-permute-start.8) | collective-permute-done | bytes 131104 | tf_op jit(solution)/shard_map/ppermute | solution.py:315
  63.5 3.5 %collective-permute-start.9 = (bf16[16,4096]{1,0:T(8,128)(2,1)S(1)}, bf16[16,4096]{1,0:T(8,128)(2,1)S(1)}, u32[]{:S(2)}, u32[]{:S(2)}) collective-permute-start(bf16[16,4096]{1,0:T(8,128)(2,1)S(1)} %add.12.refs_0_), channel_id=1, source_target_pairs={{0,96},{16,112},{32,64},{48,80},{64,32},{80,48},{96,0},{112,16},{1... | collective-permute-start | bytes 393224 | tf_op jit(solution)/shard_map/ppermute | solution.py:315
  66.9 2.8 %collective-permute-done.9.refs_1_ = bf16[16,4096]{1,0:T(8,128)(2,1)S(1)} collective-permute-done((bf16[16,4096]{1,0:T(8,128)(2,1)S(1)}, bf16[16,4096]{1,0:T(8,128)(2,1)S(1)}, u32[]{:S(2)}, u32[]{:S(2)}) %collective-permute-start.9) | collective-permute-done | bytes 131104 | tf_op jit(solution)/shard_map/ppermute | solution.py:315
  69.7 2.0 %collective-permute-start.10 = (bf16[16,4096]{1,0:T(8,128)(2,1)S(1)}, bf16[16,4096]{1,0:T(8,128)(2,1)S(1)}, u32[]{:S(2)}, u32[]{:S(2)}) collective-permute-start(bf16[16,4096]{1,0:T(8,128)(2,1)S(1)} %add.13.refs_1_), channel_id=1, source_target_pairs={{0,16},{16,0},{32,48},{48,32},{64,80},{80,64},{96,112},{112,96},{1... | collective-permute-start | bytes 393224 | tf_op jit(solution)/shard_map/ppermute | solution.py:309
  71.7 0.0 collective-permute-done.2.refs_2_
  71.7 1.0 collective-permute-done.10.refs_4_.refs_2_
  72.7 0.0 collective-permute-done.7.refs_3_
  72.7 1.0 own_x.1
  73.7 0.0 collective-permute-done.13.refs_2_
  73.7 0.0 collective-permute-done.14.refs_3_
  73.7 1.1 own_y.1
  74.8 2.0 %collective-permute-start.16 = (bf16[640,256]{1,0:T(8,128)(2,1)S(1)}, bf16[640,256]{1,0:T(8,128)(2,1)S(1)}, u32[]{:S(2)}, u32[]{:S(2)}) collective-permute-start(bf16[640,256]{1,0:T(8,128)(2,1)S(1)} %get-tuple-element.53), channel_id=1, source_target_pairs={{0,16},{16,0},{32,48},{48,32},{64,80},{80,64},{96,112},{112,96},{1... | collective-permute-start | bytes 983048 | tf_op jit(solution)/shard_map/ppermute | solution.py:309
  76.9 0.1 collective-permute-start.12
  76.9 3.9 %ortho.1.refs_0_.left_ref = bf16[32,4096]{1,0:T(8,128)(2,1)S(1)} custom-call(s32[3]{0:T(128)S(1)} %pad_add_fusion.place_ref.refs_0_, bf16[16,4096]{1,0:T(8,128)(2,1)S(1)} %add.13.refs_1_, bf16[16,4096]{1,0:T(8,128)(2,1)S(1)} %collective-permute-done.10.refs_4_.refs_2_, bf16[640,256]{1,0:T(8,128)(2,1)S(1)} %get-tuple-element.50.refs_3_.refs_4_), custom_call_target="tpu_custom_call" | custom-call | flops 1 | bytes 1 | tf_op jit(solution)/shard_map/ortho/pallas_call | solution.py:353
  80.8 1.3 %right.1.refs_2_.refs_0_ = bf16[32,896]{1,0:T(8,128)(2,1)S(1)} custom-call(bf16[32,4096]{1,0:T(8,128)(2,1)S(1)} %ortho.1.refs_0_.left_ref, bf16[4096,896]{1,0:T(8,128)(2,1)S(1)} %get-tuple-element.51.refs_1_.high_ref), custom_call_target="tpu_custom_call" | custom-call | flops 1 | bytes 1 | tf_op jit(solution)/shard_map/right/pallas_call | solution.py:373
  82.1 0.0 collective-permute-done.16.refs_1_
  82.2 1.7 %collective-permute-start.17 = (bf16[2,640,256]{2,1,0:T(8,128)(2,1)S(1)}, bf16[2,640,256]{2,1,0:T(8,128)(2,1)S(1)}, u32[]{:S(2)}, u32[]{:S(2)}) collective-permute-start(bf16[2,640,256]{2,1,0:T(8,128)(2,1)S(1)} %pack.3), channel_id=1, source_target_pairs={{0,1},{1,2},{2,3},{3,0},{4,5},{5,6},{6,7},{7,4},{8,9},{9,10},{10,1... | collective-permute-start | bytes 1966088 | tf_op jit(solution)/shard_map/ppermute | solution.py:438
  83.9 0.0 collective-permute-done.12.refs_1_
  83.9 0.4 collective-permute-start.15
  84.3 1.3 %collective-permute-start.18 = (bf16[32,896]{1,0:T(8,128)(2,1)S(1)}, bf16[32,896]{1,0:T(8,128)(2,1)S(1)}, u32[]{:S(2)}, u32[]{:S(2)}) collective-permute-start(bf16[32,896]{1,0:T(8,128)(2,1)S(1)} %right.1.refs_2_.refs_0_), channel_id=1, source_target_pairs={{0,32},{16,48},{32,0},{48,16},{64,96},{80,112},{96,64},{112,80},{1... | collective-permute-start | bytes 172040 | tf_op jit(solution)/shard_map/ppermute | solution.py:315
  85.7 2.1 %collective-permute-done.18.refs_1_ = bf16[32,896]{1,0:T(8,128)(2,1)S(1)} collective-permute-done((bf16[32,896]{1,0:T(8,128)(2,1)S(1)}, bf16[32,896]{1,0:T(8,128)(2,1)S(1)}, u32[]{:S(2)}, u32[]{:S(2)}) %collective-permute-start.18) | collective-permute-done | bytes 57376 | tf_op jit(solution)/shard_map/ppermute | solution.py:315
  87.9 3.9 %collective-permute-start.19 = (bf16[32,896]{1,0:T(8,128)(2,1)S(1)}, bf16[32,896]{1,0:T(8,128)(2,1)S(1)}, u32[]{:S(2)}, u32[]{:S(2)}) collective-permute-start(bf16[32,896]{1,0:T(8,128)(2,1)S(1)} %add.14.refs_0_), channel_id=1, source_target_pairs={{0,96},{16,112},{32,64},{48,80},{64,32},{80,48},{96,0},{112,16},{1... | collective-permute-start | bytes 172040 | tf_op jit(solution)/shard_map/ppermute | solution.py:315
  91.7 2.1 %collective-permute-done.19.refs_1_ = bf16[32,896]{1,0:T(8,128)(2,1)S(1)} collective-permute-done((bf16[32,896]{1,0:T(8,128)(2,1)S(1)}, bf16[32,896]{1,0:T(8,128)(2,1)S(1)}, u32[]{:S(2)}, u32[]{:S(2)}) %collective-permute-start.19) | collective-permute-done | bytes 57376 | tf_op jit(solution)/shard_map/ppermute | solution.py:315
  93.9 0.8 collective-permute-start.20
  94.7 0.9 collective-permute-done.20.theirs
  95.6 0.0 collective-permute-done.17.refs_6_
  95.6 0.0 collective-permute-done.15.refs_2_
  95.6 0.4 collective-permute-start.21
  95.9 0.2 collective-permute-start.23
  96.1 1.8 %collective-permute-start.22 = (bf16[640,256]{1,0:T(8,128)(2,1)S(1)}, bf16[640,256]{1,0:T(8,128)(2,1)S(1)}, u32[]{:S(2)}, u32[]{:S(2)}) collective-permute-start(bf16[640,256]{1,0:T(8,128)(2,1)S(1)} %get-tuple-element.55), channel_id=1, source_target_pairs={{0,2},{1,3},{2,0},{3,1},{4,6},{5,7},{6,4},{7,5},{8,10},{9,11},{10,... | collective-permute-start | bytes 983048 | tf_op jit(solution)/shard_map/ppermute | solution.py:430
  97.9 1.1 %collective-permute-start.11 = (bf16[640,256]{1,0:T(8,128)(2,1)S(1)}, bf16[640,256]{1,0:T(8,128)(2,1)S(1)}, u32[]{:S(2)}, u32[]{:S(2)}) collective-permute-start(bf16[640,256]{1,0:T(8,128)(2,1)S(1)} %get-tuple-element.45), channel_id=1, source_target_pairs={{0,8},{1,9},{2,10},{3,11},{4,12},{5,13},{6,14},{7,15},{8,0},{9,1},... | collective-permute-start | bytes 983048 | tf_op jit(solution)/shard_map/ppermute | solution.py:430
  99.0 4.2 %error.1 = (f32[32,896]{1,0:T(8,128)}, bf16[1,4096,896]{2,1,0:T(8,128)(2,1)}) custom-call(bf16[32,4096]{1,0:T(8,128)(2,1)S(1)} %ortho.1.refs_0_.left_ref, bf16[4096,896]{1,0:T(8,128)(2,1)S(1)} %get-tuple-element.51.refs_1_.high_ref, bf16[4096,896]{1,0:T(8,128)(2,1)S(1)} %get-tuple-element.57.low_ref, bf16[32,896]{1,0:T(8,128)(2,1)S(1)} %add.15.mine, ...), custom_call_target="tpu_custom_call" | custom-call | flops 1 | bytes 1 | tf_op jit(solution)/shard_map/error/pallas_call | solution.py:402
  103.3 3.3 %collective-permute-done.22.refs_5_ = bf16[640,256]{1,0:T(8,128)(2,1)S(1)} collective-permute-done((bf16[640,256]{1,0:T(8,128)(2,1)S(1)}, bf16[640,256]{1,0:T(8,128)(2,1)S(1)}, u32[]{:S(2)}, u32[]{:S(2)}) %collective-permute-start.22) | collective-permute-done | bytes 327712 | tf_op jit(solution)/shard_map/ppermute | solution.py:430
  106.5 1.5 %collective-permute-done.11.refs_1_ = bf16[640,256]{1,0:T(8,128)(2,1)S(1)} collective-permute-done((bf16[640,256]{1,0:T(8,128)(2,1)S(1)}, bf16[640,256]{1,0:T(8,128)(2,1)S(1)}, u32[]{:S(2)}, u32[]{:S(2)}) %collective-permute-start.11) | collective-permute-done | bytes 327712 | tf_op jit(solution)/shard_map/ppermute | solution.py:430
  108.1 0.0 collective-permute-done.21.refs_3_
  108.1 0.0 collective-permute-done.23.refs_7_
  108.1 1.2 %add_terms.1 = bf16[1280,256]{1,0:T(8,128)(2,1)} custom-call(bf16[640,256]{1,0:T(8,128)(2,1)S(1)} %get-tuple-element.44.refs_4_.refs_0_, bf16[640,256]{1,0:T(8,128)(2,1)S(1)} %collective-permute-done.11.refs_1_, bf16[2,640,256]{2,1,0:T(8,128)(2,1)S(1)} %collective-permute-done.15.refs_2_, bf16[2,640,256]{2,1,0:T(8,128)(2,1)S(1)} %collective-permute-done.21.refs_3_, ...), custom_call_target="tpu_custom_call" | custom-call | flops 1 | bytes 1 | tf_op jit(solution)/shard_map/add_terms/pallas_call | solution.py:484
  (6 shorter events, 0.2 us)
Async XLA Ops:
  19.4 13.0 %collective-permute-start.1 = (bf16[1280,896]{1,0:T(8,128)(2,1)S(1)}, bf16[1280,896]{1,0:T(8,128)(2,1)S(1)}, u32[]{:S(2)}, u32[]{:S(2)}) collective-permute-start(bf16[1280,896]{1,0:T(8,128)(2,1)S(1)} %get-tuple-element.32.grad_ref.refs_1_), channel_id=1, source_target_pairs={{0,16},{16,0},{32,48},{48,32},{64,80},{80,64},{96,112},{112,96},{1... | collective-permute-start | bytes 6881288 | tf_op jit(solution)/shard_map/ppermute | solution.py:309
  20.9 32.6 %collective-permute-start = (bf16[4,640,256]{2,1,0:T(8,128)(2,1)S(1)}, bf16[4,640,256]{2,1,0:T(8,128)(2,1)S(1)}, u32[]{:S(2)}, u32[]{:S(2)}) collective-permute-start(bf16[4,640,256]{2,1,0:T(8,128)(2,1)S(1)} %get-tuple-element.36), channel_id=1, source_target_pairs={{0,1},{1,2},{2,3},{3,0},{4,5},{5,6},{6,7},{7,4},{8,9},{9,10},{10,1... | collective-permute-start | bytes 3932168 | tf_op jit(solution)/shard_map/ppermute | solution.py:438
  23.5 31.8 %collective-permute-start.6 = (bf16[4,640,256]{2,1,0:T(8,128)(2,1)S(1)}, bf16[4,640,256]{2,1,0:T(8,128)(2,1)S(1)}, u32[]{:S(2)}, u32[]{:S(2)}) collective-permute-start(bf16[4,640,256]{2,1,0:T(8,128)(2,1)S(1)} %get-tuple-element.41), channel_id=1, source_target_pairs={{0,4},{1,5},{2,6},{3,7},{4,8},{5,9},{6,10},{7,11},{8,12},{9,13},{1... | collective-permute-start | bytes 3932168 | tf_op jit(solution)/shard_map/ppermute | solution.py:438
  32.4 4.6 %copy-start = (f32[896,32]{0,1:T(8,128)S(1)}, f32[896,32]{0,1:T(8,128)}, u32[]{:S(2)}) copy-start(f32[896,32]{0,1:T(8,128)} %param.12) | copy-start | bytes 344068
  35.8 20.4 %collective-permute-start.3 = (bf16[4,640,256]{2,1,0:T(8,128)(2,1)S(1)}, bf16[4,640,256]{2,1,0:T(8,128)(2,1)S(1)}, u32[]{:S(2)}, u32[]{:S(2)}) collective-permute-start(bf16[4,640,256]{2,1,0:T(8,128)(2,1)S(1)} %get-tuple-element.37.refs_4_), channel_id=1, source_target_pairs={{0,1},{1,2},{2,3},{3,0},{4,5},{5,6},{6,7},{7,4},{8,9},{9,10},{10,1... | collective-permute-start | bytes 3932168 | tf_op jit(solution)/shard_map/ppermute | solution.py:438
  36.5 19.8 %collective-permute-start.4 = (bf16[4,640,256]{2,1,0:T(8,128)(2,1)S(1)}, bf16[4,640,256]{2,1,0:T(8,128)(2,1)S(1)}, u32[]{:S(2)}, u32[]{:S(2)}) collective-permute-start(bf16[4,640,256]{2,1,0:T(8,128)(2,1)S(1)} %get-tuple-element.39), channel_id=1, source_target_pairs={{0,4},{1,5},{2,6},{3,7},{4,8},{5,9},{6,10},{7,11},{8,12},{9,13},{1... | collective-permute-start | bytes 3932168 | tf_op jit(solution)/shard_map/ppermute | solution.py:438
  53.4 2.2 %collective-permute-start.5 = (bf16[32,4096]{1,0:T(8,128)(2,1)S(1)}, bf16[32,4096]{1,0:T(8,128)(2,1)S(1)}, u32[]{:S(2)}, u32[]{:S(2)}) collective-permute-start(bf16[32,4096]{1,0:T(8,128)(2,1)S(1)} %get-tuple-element.38.refs_2_.refs_1_), channel_id=1, source_target_pairs={{0,16},{16,0},{32,48},{48,32},{64,80},{80,64},{96,112},{112,96},{1... | collective-permute-start | bytes 786440 | tf_op jit(solution)/shard_map/ppermute | solution.py:309
  53.8 17.9 %collective-permute-start.2 = (bf16[4,640,256]{2,1,0:T(8,128)(2,1)S(1)}, bf16[4,640,256]{2,1,0:T(8,128)(2,1)S(1)}, u32[]{:S(2)}, u32[]{:S(2)}) collective-permute-start(bf16[4,640,256]{2,1,0:T(8,128)(2,1)S(1)} %add.10.refs_2_), channel_id=1, source_target_pairs={{0,1},{1,2},{2,3},{3,0},{4,5},{5,6},{6,7},{7,4},{8,9},{9,10},{10,1... | collective-permute-start | bytes 3932168 | tf_op jit(solution)/shard_map/ppermute | solution.py:438
  56.3 16.4 %collective-permute-start.7 = (bf16[4,640,256]{2,1,0:T(8,128)(2,1)S(1)}, bf16[4,640,256]{2,1,0:T(8,128)(2,1)S(1)}, u32[]{:S(2)}, u32[]{:S(2)}) collective-permute-start(bf16[4,640,256]{2,1,0:T(8,128)(2,1)S(1)} %collective-permute-done.3), channel_id=1, source_target_pairs={{0,16},{16,0},{32,48},{48,32},{64,80},{80,64},{96,112},{112,96},{1... | collective-permute-start | bytes 3932168 | tf_op jit(solution)/shard_map/ppermute | solution.py:309
  56.6 17.1 %collective-permute-start.13 = (bf16[4,640,256]{2,1,0:T(8,128)(2,1)S(1)}, bf16[4,640,256]{2,1,0:T(8,128)(2,1)S(1)}, u32[]{:S(2)}, u32[]{:S(2)}) collective-permute-start(bf16[4,640,256]{2,1,0:T(8,128)(2,1)S(1)} %add.11.refs_3_), channel_id=1, source_target_pairs={{0,4},{1,5},{2,6},{3,7},{4,8},{5,9},{6,10},{7,11},{8,12},{9,13},{1... | collective-permute-start | bytes 3932168 | tf_op jit(solution)/shard_map/ppermute | solution.py:438
  57.9 15.8 %collective-permute-start.14 = (bf16[4,640,256]{2,1,0:T(8,128)(2,1)S(1)}, bf16[4,640,256]{2,1,0:T(8,128)(2,1)S(1)}, u32[]{:S(2)}, u32[]{:S(2)}) collective-permute-start(bf16[4,640,256]{2,1,0:T(8,128)(2,1)S(1)} %collective-permute-done.4), channel_id=1, source_target_pairs={{0,16},{16,0},{32,48},{48,32},{64,80},{80,64},{96,112},{112,96},{1... | collective-permute-start | bytes 3932168 | tf_op jit(solution)/shard_map/ppermute | solution.py:309
  58.2 5.2 %collective-permute-start.8 = (bf16[16,4096]{1,0:T(8,128)(2,1)S(1)}, bf16[16,4096]{1,0:T(8,128)(2,1)S(1)}, u32[]{:S(2)}, u32[]{:S(2)}) collective-permute-start(bf16[16,4096]{1,0:T(8,128)(2,1)S(1)} %pair_sum.1.refs_0_), channel_id=1, source_target_pairs={{0,32},{16,48},{32,0},{48,16},{64,96},{80,112},{96,64},{112,80},{1... | collective-permute-start | bytes 393224 | tf_op jit(solution)/shard_map/ppermute | solution.py:315
  63.5 6.3 %collective-permute-start.9 = (bf16[16,4096]{1,0:T(8,128)(2,1)S(1)}, bf16[16,4096]{1,0:T(8,128)(2,1)S(1)}, u32[]{:S(2)}, u32[]{:S(2)}) collective-permute-start(bf16[16,4096]{1,0:T(8,128)(2,1)S(1)} %add.12.refs_0_), channel_id=1, source_target_pairs={{0,96},{16,112},{32,64},{48,80},{64,32},{80,48},{96,0},{112,16},{1... | collective-permute-start | bytes 393224 | tf_op jit(solution)/shard_map/ppermute | solution.py:315
  69.7 2.9 %collective-permute-start.10 = (bf16[16,4096]{1,0:T(8,128)(2,1)S(1)}, bf16[16,4096]{1,0:T(8,128)(2,1)S(1)}, u32[]{:S(2)}, u32[]{:S(2)}) collective-permute-start(bf16[16,4096]{1,0:T(8,128)(2,1)S(1)} %add.13.refs_1_), channel_id=1, source_target_pairs={{0,16},{16,0},{32,48},{48,32},{64,80},{80,64},{96,112},{112,96},{1... | collective-permute-start | bytes 393224 | tf_op jit(solution)/shard_map/ppermute | solution.py:309
  74.8 7.3 %collective-permute-start.16 = (bf16[640,256]{1,0:T(8,128)(2,1)S(1)}, bf16[640,256]{1,0:T(8,128)(2,1)S(1)}, u32[]{:S(2)}, u32[]{:S(2)}) collective-permute-start(bf16[640,256]{1,0:T(8,128)(2,1)S(1)} %get-tuple-element.53), channel_id=1, source_target_pairs={{0,16},{16,0},{32,48},{48,32},{64,80},{80,64},{96,112},{112,96},{1... | collective-permute-start | bytes 983048 | tf_op jit(solution)/shard_map/ppermute | solution.py:309
  76.9 7.0 %collective-permute-start.12 = (bf16[640,256]{1,0:T(8,128)(2,1)S(1)}, bf16[640,256]{1,0:T(8,128)(2,1)S(1)}, u32[]{:S(2)}, u32[]{:S(2)}) collective-permute-start(bf16[640,256]{1,0:T(8,128)(2,1)S(1)} %get-tuple-element.47), channel_id=1, source_target_pairs={{0,16},{16,0},{32,48},{48,32},{64,80},{80,64},{96,112},{112,96},{1... | collective-permute-start | bytes 983048 | tf_op jit(solution)/shard_map/ppermute | solution.py:309
  82.2 13.4 %collective-permute-start.17 = (bf16[2,640,256]{2,1,0:T(8,128)(2,1)S(1)}, bf16[2,640,256]{2,1,0:T(8,128)(2,1)S(1)}, u32[]{:S(2)}, u32[]{:S(2)}) collective-permute-start(bf16[2,640,256]{2,1,0:T(8,128)(2,1)S(1)} %pack.3), channel_id=1, source_target_pairs={{0,1},{1,2},{2,3},{3,0},{4,5},{5,6},{6,7},{7,4},{8,9},{9,10},{10,1... | collective-permute-start | bytes 1966088 | tf_op jit(solution)/shard_map/ppermute | solution.py:438
  83.9 11.7 %collective-permute-start.15 = (bf16[2,640,256]{2,1,0:T(8,128)(2,1)S(1)}, bf16[2,640,256]{2,1,0:T(8,128)(2,1)S(1)}, u32[]{:S(2)}, u32[]{:S(2)}) collective-permute-start(bf16[2,640,256]{2,1,0:T(8,128)(2,1)S(1)} %pack.2), channel_id=1, source_target_pairs={{0,4},{1,5},{2,6},{3,7},{4,8},{5,9},{6,10},{7,11},{8,12},{9,13},{1... | collective-permute-start | bytes 1966088 | tf_op jit(solution)/shard_map/ppermute | solution.py:438
  84.3 3.5 %collective-permute-start.18 = (bf16[32,896]{1,0:T(8,128)(2,1)S(1)}, bf16[32,896]{1,0:T(8,128)(2,1)S(1)}, u32[]{:S(2)}, u32[]{:S(2)}) collective-permute-start(bf16[32,896]{1,0:T(8,128)(2,1)S(1)} %right.1.refs_2_.refs_0_), channel_id=1, source_target_pairs={{0,32},{16,48},{32,0},{48,16},{64,96},{80,112},{96,64},{112,80},{1... | collective-permute-start | bytes 172040 | tf_op jit(solution)/shard_map/ppermute | solution.py:315
  87.9 6.0 %collective-permute-start.19 = (bf16[32,896]{1,0:T(8,128)(2,1)S(1)}, bf16[32,896]{1,0:T(8,128)(2,1)S(1)}, u32[]{:S(2)}, u32[]{:S(2)}) collective-permute-start(bf16[32,896]{1,0:T(8,128)(2,1)S(1)} %add.14.refs_0_), channel_id=1, source_target_pairs={{0,96},{16,112},{32,64},{48,80},{64,32},{80,48},{96,0},{112,16},{1... | collective-permute-start | bytes 172040 | tf_op jit(solution)/shard_map/ppermute | solution.py:315
  93.9 1.7 %collective-permute-start.20 = (bf16[32,896]{1,0:T(8,128)(2,1)S(1)}, bf16[32,896]{1,0:T(8,128)(2,1)S(1)}, u32[]{:S(2)}, u32[]{:S(2)}) collective-permute-start(bf16[32,896]{1,0:T(8,128)(2,1)S(1)} %add.15.mine), channel_id=1, source_target_pairs={{0,16},{16,0},{32,48},{48,32},{64,80},{80,64},{96,112},{112,96},{1... | collective-permute-start | bytes 172040 | tf_op jit(solution)/shard_map/ppermute | solution.py:309
  95.6 12.5 %collective-permute-start.21 = (bf16[2,640,256]{2,1,0:T(8,128)(2,1)S(1)}, bf16[2,640,256]{2,1,0:T(8,128)(2,1)S(1)}, u32[]{:S(2)}, u32[]{:S(2)}) collective-permute-start(bf16[2,640,256]{2,1,0:T(8,128)(2,1)S(1)} %collective-permute-done.15.refs_2_), channel_id=1, source_target_pairs={{0,16},{16,0},{32,48},{48,32},{64,80},{80,64},{96,112},{112,96},{1... | collective-permute-start | bytes 1966088 | tf_op jit(solution)/shard_map/ppermute | solution.py:309
  95.9 12.1 %collective-permute-start.23 = (bf16[2,640,256]{2,1,0:T(8,128)(2,1)S(1)}, bf16[2,640,256]{2,1,0:T(8,128)(2,1)S(1)}, u32[]{:S(2)}, u32[]{:S(2)}) collective-permute-start(bf16[2,640,256]{2,1,0:T(8,128)(2,1)S(1)} %collective-permute-done.17.refs_6_), channel_id=1, source_target_pairs={{0,16},{16,0},{32,48},{48,32},{64,80},{80,64},{96,112},{112,96},{1... | collective-permute-start | bytes 1966088 | tf_op jit(solution)/shard_map/ppermute | solution.py:309
  96.1 10.5 %collective-permute-start.22 = (bf16[640,256]{1,0:T(8,128)(2,1)S(1)}, bf16[640,256]{1,0:T(8,128)(2,1)S(1)}, u32[]{:S(2)}, u32[]{:S(2)}) collective-permute-start(bf16[640,256]{1,0:T(8,128)(2,1)S(1)} %get-tuple-element.55), channel_id=1, source_target_pairs={{0,2},{1,3},{2,0},{3,1},{4,6},{5,7},{6,4},{7,5},{8,10},{9,11},{10,... | collective-permute-start | bytes 983048 | tf_op jit(solution)/shard_map/ppermute | solution.py:430
  97.9 10.1 %collective-permute-start.11 = (bf16[640,256]{1,0:T(8,128)(2,1)S(1)}, bf16[640,256]{1,0:T(8,128)(2,1)S(1)}, u32[]{:S(2)}, u32[]{:S(2)}) collective-permute-start(bf16[640,256]{1,0:T(8,128)(2,1)S(1)} %get-tuple-element.45), channel_id=1, source_target_pairs={{0,8},{1,9},{2,10},{3,11},{4,12},{5,13},{6,14},{7,15},{8,0},{9,1},... | collective-permute-start | bytes 983048 | tf_op jit(solution)/shard_map/ppermute | solution.py:430
